TPU v7x, 128 devices: a whole 4x4x4 slice. The times are simulated.
128 devices in a mesh: rep: 8 (over z, y_hi), expert: 16 (over y_lo, x, core).
Axes of the slice: x: 4, y: 4 (y_hi: 2, y_lo: 2; y = y_hi * 2 + y_lo), z: 4, core: 2. Of those that a mesh axis runs over, the one named last changes fastest.
Arguments:
- tokens: bfloat16 [16384, 2048], P(('rep', 'expert')), may hold values from -6 to 6
- norm_gain: float32 [2048], replicated, may hold values from 0.1 to 1.9
- router: bfloat16 [2048, 128], P('rep'), may hold values from -0.125 to 0.125
- routes: int32 [16384, 8], P(('rep', 'expert')), may hold values from 0 to 127, all different within a row; in each aligned block of 128 rows (0 to 127, 128 to 255, ...) at most 12 rows name the same one
- placement: int32 [128], replicated, may hold values from 0 to 127, each once
- w_gate: bfloat16 [128, 2048, 768], P(('rep', 'expert')), may hold values from -0.125 to 0.125
- w_up: bfloat16 [128, 2048, 768], P(('rep', 'expert')), may hold values from -0.125 to 0.125
- w_down: bfloat16 [128, 768, 2048], P(('rep', 'expert')), may hold values from -0.21875 to 0.21875
Outputs:
- moe_out: bfloat16 [16384, 2048], P(('rep', 'expert'))
Inputs may be any that keep to these rules, and one draw needn't show every extreme that they name: `routes`: each token's 8 experts differ. Among the 128 tokens of one device at most 12 rows name any one expert, and in some devices' rows one expert is named exactly 12 times. `placement`: A permutation. Weight slot s lies on the device numbered s over rep then expert.
All inputs are finite; a program needn't handle non-finite values.
Results may differ from a plain program's by a relative error of at most 0.0075.
Values may be sent and summed in bfloat16 or wider, within the bound.
A program may use at most 128 MiB of HBM per device.

v0:
```python
import jax
import jax.numpy as jnp
from jax import lax
from jax.sharding import PartitionSpec as P


def per_device(tokens, norm_gain, router, routes, placement, w_gate, w_up, w_down):
    tok_rows = tokens.shape[0]
    model_width = tokens.shape[1]
    top_count = routes.shape[1]
    expert_count = placement.shape[0]
    rep_count = lax.axis_size("rep")
    owner_count = lax.axis_size("expert")
    devices = rep_count * owner_count
    capacity = 3 * tok_rows * top_count // (2 * expert_count)
    values = tokens.astype(jnp.float32)
    scale = lax.rsqrt(jnp.mean(values * values, axis=-1, keepdims=True) + 1e-06)
    normed = (values * scale * norm_gain[None, :]).astype(jnp.bfloat16)
    logits = jnp.dot(
        normed,
        lax.all_gather(router, "rep", axis=0, tiled=True),
        preferred_element_type=jnp.float32,
    )
    picked = jnp.take_along_axis(logits, routes, axis=1)
    powers = jnp.exp(picked)
    shares = (powers / jnp.sum(powers, axis=1, keepdims=True)).reshape(-1)
    flat_routes = routes.reshape(-1)
    one_hot = (flat_routes[:, None] == jnp.arange(expert_count, dtype=jnp.int32)[None, :]).astype(
        jnp.int32
    )
    target = jnp.sum(one_hot * placement[None, :], axis=1)
    earlier = jnp.cumsum(one_hot, axis=0) - one_hot
    slot_rank = jnp.sum(earlier * one_hot, axis=1)
    position = target * capacity + slot_rank
    repeated = jnp.repeat(normed, top_count, axis=0)
    outgoing = jnp.zeros((devices * capacity, model_width), jnp.bfloat16).at[position].set(repeated)
    outgoing = outgoing.reshape(devices, capacity, model_width)
    received = lax.all_to_all(outgoing, ("rep", "expert"), split_axis=0, concat_axis=0, tiled=True)
    stacked = received.reshape(-1, model_width)
    gate_proj = jnp.dot(stacked, w_gate[0], preferred_element_type=jnp.float32)
    up_proj = jnp.dot(stacked, w_up[0], preferred_element_type=jnp.float32)
    hidden = (jax.nn.silu(gate_proj) * up_proj).astype(jnp.bfloat16)
    result = jnp.dot(hidden, w_down[0], preferred_element_type=jnp.float32).astype(jnp.bfloat16)
    returned = lax.all_to_all(
        result.reshape(received.shape), ("rep", "expert"), split_axis=0, concat_axis=0, tiled=True
    )
    collected = returned.reshape(devices * capacity, model_width)[position]
    weighted = collected.astype(jnp.float32) * shares[:, None]
    combined = jnp.sum(weighted.reshape(tok_rows, top_count, model_width), axis=1)
    return combined.astype(jnp.bfloat16)


def solution(mesh):
    placed = (
        P(("rep", "expert"), None),
        P(),
        P("rep", None),
        P(("rep", "expert"), None),
        P(),
        P(("rep", "expert"), None, None),
        P(("rep", "expert"), None, None),
        P(("rep", "expert"), None, None),
    )
    return jax.shard_map(
        per_device,
        mesh=mesh,
        in_specs=placed,
        out_specs=P(("rep", "expert"), None),
        check_vma=False,
    )
```

profile of v0, /device:TPU:0, one launch (start us, length us, event | category | flops | bytes accessed | tf_op | source)
XLA Modules:
  0.0 347.9 jit_solution(2279940456517043774)
XLA Ops:
  0.0 0.0 copy-start
  0.0 0.9 copy.19
  0.9 0.1 eq.29
  1.0 0.1 eq.25
  1.1 1.2 fusion.9
  2.4 0.1 copy.21
  2.5 0.2 fusion.14
  2.7 0.0 copy-start.4
  2.7 0.8 copy-done.4
  3.5 1.1 broadcast_add_fusion
  4.6 0.1 copy.22
  4.7 1.2 select_reduce_fusion
  5.9 2.0 fusion.11
  7.9 10.7 %scatter_custom_fusion = bf16[1536,2048]{1,0:T(8,128)(2,1)} fusion(s32[1024]{0:T(1024)S(1)} %bitcast.38, bf16[]{:T(256)} %constant.12.clone.1, bf16[128,2048]{1,0:T(8,128)(2,1)} %fusion.11), kind=kCustom, calls=%fused_computation.7 | custom fusion | bytes 6815746 | tf_op jit(solution)/shard_map/scatter | solution.py:36
  18.6 10.6 %reshape.104 = bf16[128,12,2048]{2,1,0:T(8,128)(2,1)} reshape(bf16[1536,2048]{1,0:T(8,128)(2,1)} %scatter_custom_fusion) | data formatting | bytes 12582912 | tf_op jit(solution)/shard_map/reshape | solution.py:37
  29.2 109.1 %all_to_all.10 = bf16[128,12,2048]{2,1,0:T(8,128)(2,1)} all-to-all(bf16[128,12,2048]{2,1,0:T(8,128)(2,1)} %reshape.104), channel_id=1, replica_groups=mesh['rep'=8,'expert'=16] {'rep','expert'}, dimensions={0} | all-to-all | bytes 12582912 | tf_op jit(solution)/shard_map/all_to_all | solution.py:38
  138.3 10.7 %reshape.105 = bf16[1536,2048]{1,0:T(8,128)(2,1)} reshape(bf16[128,12,2048]{2,1,0:T(8,128)(2,1)} %all_to_all.10) | data formatting | bytes 12582912 | tf_op jit(solution)/shard_map/reshape | solution.py:39
  149.0 0.0 copy-start.2
  149.0 0.0 copy-start.7
  149.0 8.2 %fusion.5 = f32[1536,768]{1,0:T(8,128)S(1)} fusion(bf16[1536,2048]{1,0:T(8,128)(2,1)} %reshape.105, bf16[1,2048,768]{2,1,0:T(8,128)(2,1)} %param.13), kind=kOutput, calls=%fused_computation.11 | convolution fusion | flops 4831838208 | bytes 14155776 | tf_op jit(solution)/shard_map/dot_general | solution.py:40
  157.2 0.0 copy-done.2
  157.2 0.0 copy-done.7
  157.2 5.6 %multiply_convert_fusion = bf16[1536,768]{1,0:T(8,128)(2,1)S(1)} fusion(f32[1536,768]{1,0:T(8,128)S(1)} %fusion.5, bf16[1536,2048]{1,0:T(8,128)(2,1)S(1)} %copy-done.2, bf16[1,2048,768]{2,1,0:T(8,128)(2,1)S(1)} %copy-done.7), kind=kOutput, calls=%fused_computation.6 | convolution fusion | flops 4838916096 | bytes 16515072 | tf_op jit(solution)/shard_map/dot_general | solution.py:41
  162.8 0.0 copy-done
  162.8 7.1 %convolution_convert_fusion = bf16[1536,2048]{1,0:T(8,128)(2,1)} fusion(bf16[1536,768]{1,0:T(8,128)(2,1)S(1)} %multiply_convert_fusion, bf16[1,768,2048]{2,1,0:T(8,128)(2,1)S(1)} %copy-done), kind=kOutput, calls=%fused_computation.5 | convolution fusion | flops 4834983936 | bytes 11796480 | tf_op jit(solution)/shard_map/dot_general | solution.py:43
  169.9 10.6 %reshape.106 = bf16[128,12,2048]{2,1,0:T(8,128)(2,1)} reshape(bf16[1536,2048]{1,0:T(8,128)(2,1)} %convolution_convert_fusion) | data formatting | bytes 12582912 | tf_op jit(solution)/shard_map/reshape | solution.py:45
  180.5 0.0 copy-start.6
  180.5 0.0 copy-start.5
  180.5 0.0 copy-start.3
  180.5 6.1 %all-to-all-start.1 = ((bf16[128,12,2048]{2,1,0:T(8,128)(2,1)}), bf16[128,12,2048]{2,1,0:T(8,128)(2,1)}, u32[]{:S(2)}, u32[]{:S(2)}) async-start(bf16[128,12,2048]{2,1,0:T(8,128)(2,1)} %reshape.106), calls=%async_computation.1 | async-start | bytes 16777216 | tf_op jit(solution)/shard_map/all_to_all | solution.py:44
  186.6 0.0 copy-done.6
  186.6 0.1 copy.23
  186.7 0.1 reshape.118
  186.8 0.0 copy-done.5
  186.8 123.1 %all_gather.3 = bf16[2048,128]{1,0:T(8,128)(2,1)S(1)} all-gather(bf16[256,128]{1,0:T(8,128)(2,1)S(1)} %copy-done.5), channel_id=1, replica_groups=mesh['rep'=8,'expert'=16] {'rep'}, dimensions={0}, use_global_device_ids=true | all-gather | bytes 589824 | tf_op jit(solution)/shard_map/all_gather | solution.py:21
  309.9 0.0 copy-done.3
  309.9 0.3 fusion.18
  310.2 6.8 %gather_fusion.1 = f32[1024]{0:T(1024)S(1)} fusion(f32[128,128]{1,0:T(8,128)S(1)} %fusion.18, s32[1024]{0:T(1024)S(1)} %reshape.118), kind=kCustom, calls=%fused_computation.1 | custom fusion | bytes 16384 | tf_op jit(solution)/shard_map/jit(take_along_axis)/gather | solution.py:24
  317.0 0.1 reshape.121
  317.1 0.1 copy.25
  317.3 0.0 all-to-all-done.1
  317.3 10.7 %reshape.107 = bf16[1536,2048]{1,0:T(8,128)(2,1)} reshape(bf16[128,12,2048]{2,1,0:T(8,128)(2,1)} %all-to-all-done.1) | data formatting | bytes 12582912 | tf_op jit(solution)/shard_map/reshape | solution.py:47
  328.0 0.0 copy-start.1
  328.0 12.6 %gather_fusion = bf16[1024,2048]{1,0:T(8,128)(2,1)} fusion(bf16[1536,2048]{1,0:T(8,128)(2,1)} %reshape.107, s32[1024]{0:T(1024)S(1)} %broadcast_clamp_fusion), kind=kCustom, calls=%fused_computation | custom fusion | bytes 8392704 | tf_op jit(solution)/shard_map/gather | solution.py:47
  340.6 7.3 %fusion = bf16[128,2048]{1,0:T(8,128)(2,1)} fusion(bf16[1024,2048]{1,0:T(8,128)(2,1)} %gather_fusion, f32[128,8]{1,0:T(8,128)S(1)} %copy.25), kind=kLoop, calls=%fused_computation.4 | loop fusion | flops 6029312 | bytes 4722688 | tf_op jit(solution)/shard_map/reduce_sum | solution.py:49
  347.9 0.0 copy-done.1
  (11 shorter events, 0.2 us)
Async XLA Ops:
  0.0 162.8 %copy-start = (bf16[1,768,2048]{2,1,0:T(8,128)(2,1)S(1)}, bf16[1,768,2048]{2,1,0:T(8,128)(2,1)}, u32[]{:S(2)}) copy-start(bf16[1,768,2048]{2,1,0:T(8,128)(2,1)} %param.15) | copy-start | bytes 9437188
  2.7 0.8 copy-start.4
  149.0 8.2 %copy-start.2 = (bf16[1536,2048]{1,0:T(8,128)(2,1)S(1)}, bf16[1536,2048]{1,0:T(8,128)(2,1)}, u32[]{:S(2)}) copy-start(bf16[1536,2048]{1,0:T(8,128)(2,1)} %reshape.105) | copy-start | bytes 18874372
  149.0 8.2 %copy-start.7 = (bf16[1,2048,768]{2,1,0:T(8,128)(2,1)S(1)}, bf16[1,2048,768]{2,1,0:T(8,128)(2,1)}, u32[]{:S(2)}) copy-start(bf16[1,2048,768]{2,1,0:T(8,128)(2,1)} %param.14) | copy-start | bytes 9437188
  180.5 6.1 %copy-start.6 = (s32[128,8]{0,1:T(8,128)S(1)}, s32[128,8]{0,1:T(8,128)}, u32[]{:S(2)}) copy-start(s32[128,8]{0,1:T(8,128)} %param.11) | copy-start | bytes 12292
  180.5 6.3 %copy-start.5 = (bf16[256,128]{1,0:T(8,128)(2,1)S(1)}, bf16[256,128]{1,0:T(8,128)(2,1)}, u32[]{:S(2)}) copy-start(bf16[256,128]{1,0:T(8,128)(2,1)} %param.10) | copy-start | bytes 196612
  180.5 129.4 %copy-start.3 = (bf16[128,2048]{1,0:T(8,128)(2,1)S(1)}, bf16[128,2048]{1,0:T(8,128)(2,1)}, u32[]{:S(2)}) copy-start(bf16[128,2048]{1,0:T(8,128)(2,1)} %fusion.11) | copy-start | bytes 1572868
  180.5 136.8 %all-to-all-start.1 = ((bf16[128,12,2048]{2,1,0:T(8,128)(2,1)}), bf16[128,12,2048]{2,1,0:T(8,128)(2,1)}, u32[]{:S(2)}, u32[]{:S(2)}) async-start(bf16[128,12,2048]{2,1,0:T(8,128)(2,1)} %reshape.106), calls=%async_computation.1 | async-start | bytes 16777216 | tf_op jit(solution)/shard_map/all_to_all | solution.py:44
  328.0 19.9 %copy-start.1 = (bf16[1,768,2048]{2,1,0:T(8,128)(2,1)S(1)}, bf16[1,768,2048]{2,1,0:T(8,128)(2,1)}, u32[]{:S(2)}) copy-start(bf16[1,768,2048]{2,1,0:T(8,128)(2,1)} %param.15) | copy-start | bytes 9437188
where the time goes:
time: 353 us; the launch traced here: 348 us
  blocking collectives  232 us (66%)
  local copies, waits for them, and re-layouts  75.2 us (21%)
  matrix products  21.2 us (6%)
  other arithmetic  13.1 us (4%)
  starting transfers between devices  6.07 us (2%)
    all_gather x1, blocking collectives, per_device(): lax.all_gather(router, 'rep', axis=0, tiled=True)  123 us
    all_to_all x1, blocking collectives, per_device(): lax.all_to_all(outgoing, ('rep', 'expert'), split_axis=0, concat_axis=0,...  109 us
    gather x1, local copies, waits for them, and re-layouts, per_device(): collected = returned.reshape(devices * capacity, model_width)[position]  12.6 us
    reshape x1, local copies, waits for them, and re-layouts, per_device(): collected = returned.reshape(devices * capacity, model_width)[position]  10.7 us
    scatter x1, local copies, waits for them, and re-layouts, per_device(): jnp.zeros((devices * capacity, model_width), jnp.bfloat16).at[position]  10.7 us
    reshape x1, local copies, waits for them, and re-layouts, per_device(): stacked = received.reshape(-1, model_width)  10.7 us
    reshape x1, local copies, waits for them, and re-layouts, per_device(): outgoing = outgoing.reshape(devices, capacity, model_width)  10.6 us
    reshape x1, local copies, waits for them, and re-layouts, per_device(): result.reshape(received.shape)  10.6 us
  transfers between devices with their start and end apart: 1, of which 0 were waited for; matrix products, arithmetic and copies ran while one was open for 2% of the time, Pallas kernels for 0%

commit v1 on v0

v1 whole, which is shorter than its diff:
```python
import jax
import jax.numpy as jnp
from jax import lax
from jax.experimental import pallas as pl
from jax.experimental.pallas import tpu as pltpu
from jax.sharding import PartitionSpec as P

MESH = pl.DeviceIdType.MESH
TOK = 128
WIDTH = 2048
HIDDEN = 768
SIDE = 4
ROUNDS = 3
SLOTS = 4
DEVICES = 128
GROUPS = (
    (0, 768, (0, 1, 2)),
    (768, 640, (1, 2, 0)),
    (1408, 640, (2, 0, 1)),
)
NT = (((1,), (1,)), ((), ()))


def iota(shape, dim):
    return lax.broadcasted_iota(jnp.int32, shape, dim)


def dot(a, b):
    return jnp.dot(a, b, preferred_element_type=jnp.float32)


def dot_nt(a, b):
    return lax.dot_general(a, b, NT, preferred_element_type=jnp.float32)


def kernel(
    tokens, gain, router, routes, placement, w_gate, w_up, w_down, out,
    blocks, ranks, weights, packed, hop2, arrived, back3, back2, back1, total,
    gate_v, up_v, down_v, normed, table, stacked, hidden, slot_of, rank_x, share_x,
    w_sem, t_send, t_recv, s1_send, s1_recv, q_send, q_recv, p_send, p_recv,
    s2_send, s2_recv, s3_send, s3_recv, r3_send, r3_recv, r2_send, r2_recv, r1_send, r1_recv,
):
    rep = lax.axis_index("rep")
    exp = lax.axis_index("expert")
    core = exp % 2
    at = (rep // 2, (rep % 2) * 2 + exp // 8, (exp // 2) % 4)

    def device(pos, c):
        z, y, x = pos
        return (z * 2 + y // 2, (y % 2) * 8 + x * 2 + c)

    def along(axis, value, c):
        pos = list(at)
        pos[axis] = value
        return device(pos, c)

    def near(axis, step):
        return (at[axis] + step) % SIDE

    def remote(src, dst, send, recv, dev):
        return pltpu.make_async_remote_copy(
            src_ref=src, dst_ref=dst, send_sem=send, recv_sem=recv,
            device_id=dev, device_id_type=MESH,
        )

    loads = [
        pltpu.make_async_copy(w_gate.at[0], gate_v, w_sem.at[0]),
        pltpu.make_async_copy(w_up.at[0], up_v, w_sem.at[1]),
        pltpu.make_async_copy(w_down.at[0], down_v, w_sem.at[2]),
    ]
    for load in loads:
        load.start()

    barrier = pltpu.get_barrier_semaphore()
    greeted = [along(a, near(a, i), (core + d) % 2) for a in range(3) for i in (1, 2, 3) for d in (0, 1)]
    greeted.append(device(at, 1 - core))
    greeted += [device((near(0, i), near(1, 2), at[2]), core) for i in (1, 2, 3)]
    for dev in greeted:
        pl.semaphore_signal(barrier, inc=1, device_id=dev, device_id_type=MESH)

    values = tokens[...].astype(jnp.float32)
    scale = lax.rsqrt(jnp.mean(values * values, axis=-1, keepdims=True) + 1e-06)
    normed[...] = (values * scale * gain[...]).astype(jnp.bfloat16)
    for g, (first, width, axes) in enumerate(GROUPS):
        blocks[g][pl.ds(pl.multiple_of(at[axes[0]] * TOK, TOK), TOK), :] = normed[:, first:first + width]

    member = jnp.zeros((TOK, DEVICES), jnp.float32)
    lanes = iota((TOK, DEVICES), 1)
    for k in range(8):
        member = member + jnp.where(routes[:, k:k + 1] == lanes, 1.0, 0.0)
    holder = jnp.where(placement[...] == iota((DEVICES, DEVICES), 0), 1.0, 0.0).astype(jnp.bfloat16)
    by_slot = dot_nt(member.astype(jnp.bfloat16), holder)
    before = jnp.where(iota((TOK, TOK), 1) < iota((TOK, TOK), 0), 1.0, 0.0).astype(jnp.bfloat16)
    rank = jnp.where(by_slot > 0.5, dot(before, by_slot.astype(jnp.bfloat16)), -1.0).astype(jnp.bfloat16)
    for g, (first, width, axes) in enumerate(GROUPS):
        ranks[g, pl.ds(pl.multiple_of(at[axes[0]] * TOK, TOK), TOK), :] = rank
    table[pl.ds(pl.multiple_of(rep * 256, 256), 256), :] = router[...]

    pl.semaphore_wait(barrier, len(greeted))

    def own(g, where=None):
        position = at[GROUPS[g][2][0]] if where is None else where
        return pl.ds(pl.multiple_of(position * TOK, TOK), TOK)

    def s1(g, i, where=None):
        a = GROUPS[g][2][0]
        return remote(blocks[g].at[own(g)], blocks[g].at[own(g, where)], s1_send.at[g, i], s1_recv.at[g, i],
                      along(a, near(a, i), core))

    def sq(g, i, where=None):
        a = GROUPS[g][2][0]
        return remote(ranks.at[g, own(g)], ranks.at[g, own(g, where)], q_send.at[g, i], q_recv.at[g, i],
                      along(a, near(a, i), core))

    def sp(g, i, where=None):
        a = GROUPS[g][2][0]
        return remote(weights.at[g, own(g)], weights.at[g, own(g, where)], p_send.at[g, i], p_recv.at[g, i],
                      along(a, near(a, i), core))

    def shard(r):
        return table.at[pl.ds(pl.multiple_of(r * 256, 256), 256)]

    def st(i, r=None):
        return remote(shard(rep), shard(rep if r is None else r), t_send.at[i], t_recv.at[i], ((rep + i) % 8, exp))

    for g in range(3):
        for i in (2, 1, 3):
            sq(g, i).start()
    for i in (2, 1, 3):
        for g in range(3):
            s1(g, i).start()
    for i in range(1, 8):
        st(i).start()

    row = iota((TOK, SIDE * TOK), 0)
    col = iota((TOK, SIDE * TOK), 1)
    slot_of[...] = jnp.where((row // 4) % 4 == col // TOK, row % 4, 1000).astype(jnp.float32)

    def chosen(g, v):
        a1, a2, a3 = GROUPS[g][2]
        r = iota((TOK, DEVICES), 0)
        s = iota((TOK, DEVICES), 1)
        pos = [None, None, None]
        pos[a1] = at[a1]
        pos[a2] = v
        pos[a3] = r // 32
        wanted = pos[0] * 32 + pos[1] * 8 + pos[2] * 2 + (r // 16) % 2
        return jnp.where(s == wanted, 1.0, 0.0).astype(jnp.bfloat16)

    def swap(g):
        r = iota((256, 256), 0)
        c = iota((256, 256), 1)
        a, b, d, s = r // 64, (r // 16) % 4, (r // 4) % 4, r % 4
        if g == 0:
            wanted = d * 64 + b * 16 + a * 4 + s
        else:
            wanted = a * 64 + d * 16 + b * 4 + s
        return jnp.where(c == wanted, 1.0, 0.0).astype(jnp.bfloat16)

    def s2(g, q, i, where=None):
        a = GROUPS[g][2][1]
        v = near(a, i)
        return remote(packed[g].at[q, pl.ds(v * 8, 8)], hop2[g].at[q, at[a] if where is None else where],
                      s2_send.at[g, q, i], s2_recv.at[g, q, i], along(a, v, core))

    def s3(g, q, i, d, where=None):
        a = GROUPS[g][2][2]
        u, c = near(a, i), (core + d) % 2
        src = hop2[g].at[q, :, u * 2 + c]
        dst = arrived[g].at[q, core * 4 + at[a] if where is None else where]
        if i == 0 and d == 0:
            return pltpu.make_async_copy(src, dst, s3_recv.at[g, q, 0])
        return remote(src, dst, s3_send.at[g, q, i * 2 + d], s3_recv.at[g, q, i * 2 + d], along(a, u, c))

    def r3(g, q, i, d, where=None):
        a = GROUPS[g][2][2]
        u, c = near(a, i), (core + d) % 2
        src = packed[g].at[q, pl.ds((c * 4 + u) * 4, 4)]
        dst = back3[g].at[q, :, at[a] * 2 + core if where is None else where]
        if i == 0 and d == 0:
            return pltpu.make_async_copy(src, dst, r3_recv.at[g, q, 0])
        return remote(src, dst, r3_send.at[g, q, i * 2 + d], r3_recv.at[g, q, i * 2 + d], along(a, u, c))

    def r2(g, q, i, where=None):
        a = GROUPS[g][2][1]
        v = near(a, i)
        src, dst = back3[g].at[q, v], back2[g].at[q, at[a] if where is None else where]
        if i == 0:
            return pltpu.make_async_copy(src, dst, r2_recv.at[g, q, 0])
        return remote(src, dst, r2_send.at[g, q, i], r2_recv.at[g, q, i], along(a, v, core))

    def r1(g, i):
        a = GROUPS[g][2][0]
        return remote(blocks[g].at[own(g, near(a, i))], back1[g].at[i - 1], r1_send.at[g, i], r1_recv.at[g, i],
                      along(a, near(a, i), core))

    PAIRS = [(i, d) for i in (2, 1, 3, 0) for d in (0, 1)]

    def gather(q):
        slot = slot_of[...] + (q * SLOTS).astype(jnp.float32)
        for i in (2, 1, 3, 0):
            for g, (first, width, axes) in enumerate(GROUPS):
                v = near(axes[1], i)
                found = dot_nt(chosen(g, v), ranks[g])
                pick = jnp.where(found == slot, 1.0, 0.0).astype(jnp.bfloat16)
                rows = dot(pick, blocks[g][...]).astype(jnp.bfloat16).reshape(8, 16, width)
                if i == 0:
                    hop2[g][q, v] = rows
                else:
                    packed[g][q, pl.ds(v * 8, 8)] = rows
                    s2(g, q, i).start()

    def forward(q):
        for g in range(3):
            for i in (1, 2, 3):
                s2(g, q, i, near(GROUPS[g][2][1], -i)).wait_recv()
            for i, d in PAIRS:
                s3(g, q, i, d).start()

    def expert(q):
        for g, (first, width, axes) in enumerate(GROUPS):
            for i, d in PAIRS:
                copy = s3(g, q, i, d, ((core + d) % 2) * 4 + near(axes[2], -i))
                if i == 0 and d == 0:
                    copy.wait()
                else:
                    copy.wait_recv()
            for c in (0, 1):
                part = arrived[g][q, pl.ds(c * 4, 4)]
                if g == 2:
                    for y in range(4):
                        for z in range(4):
                            at_row = c * 256 + z * 64 + y * 16
                            stacked[at_row:at_row + 16, first:first + width] = part[y, z]
                else:
                    stacked[c * 256:(c + 1) * 256, first:first + width] = dot(
                        swap(g), part.reshape(256, width)).astype(jnp.bfloat16)

        def tile(n, carry):
            cols = pl.ds(pl.multiple_of(n * 256, 256), 256)
            gate = dot(stacked[...], gate_v[:, cols])
            up = dot(stacked[...], up_v[:, cols])
            hidden[:, cols] = (gate / (1.0 + jnp.exp(-gate)) * up).astype(jnp.bfloat16)
            return carry

        lax.fori_loop(0, HIDDEN // 256, tile, 0)
        for g, (first, width, axes) in enumerate(GROUPS):
            result = dot(hidden[...], down_v[:, first:first + width]).astype(jnp.bfloat16)
            for i in (1, 2, 3):
                s2(g, q, i).wait_send()
            for c in (0, 1):
                half = result[c * 256:(c + 1) * 256]
                if g == 2:
                    half = half.reshape(4, 4, 16, width)
                    for y in range(4):
                        for z in range(4):
                            packed[g][q, c * 16 + y * 4 + z] = half[z, y]
                else:
                    packed[g][q, pl.ds(c * 16, 16)] = dot(swap(g), half).astype(jnp.bfloat16).reshape(16, 16, width)
            for i, d in PAIRS:
                r3(g, q, i, d).start()

    def back(q):
        for g, (first, width, axes) in enumerate(GROUPS):
            for i, d in PAIRS:
                copy = r3(g, q, i, d, near(axes[2], -i) * 2 + (core + d) % 2)
                if i == 0 and d == 0:
                    copy.wait()
                else:
                    copy.wait_recv()
            for i in (2, 1, 3, 0):
                r2(g, q, i).start()

    def combine(q):
        for g, (first, width, axes) in enumerate(GROUPS):
            for i in (1, 2, 3):
                r2(g, q, i, near(axes[1], -i)).wait_recv()
            r2(g, q, 0).wait()
            slot = (q * SLOTS).astype(jnp.float32)
            r = iota((SIDE * TOK, SIDE * TOK), 0)
            s = iota((SIDE * TOK, SIDE * TOK), 1)
            wanted = jnp.where((s // 4) % 4 == r // TOK, s % 4, 1000).astype(jnp.float32) + slot
            mix = jnp.where(rank_x[g].astype(jnp.float32) == wanted, share_x[g].astype(jnp.float32), 0.0)
            total[g][...] += dot(mix.astype(jnp.bfloat16), back2[g][q].reshape(SIDE * TOK, width))

            @pl.when(q == ROUNDS - 1)
            def _():
                for i in (1, 2, 3):
                    s1(g, i).wait_send()
                blocks[g][...] = total[g][...].astype(jnp.bfloat16)
                for i in (2, 1, 3):
                    r1(g, i).start()

    def shares():
        for i in range(1, 8):
            st(i, (rep + 8 - i) % 8).wait_recv()
        logits = dot(normed[...], table[...])
        member = jnp.zeros((TOK, DEVICES), jnp.float32)
        lanes = iota((TOK, DEVICES), 1)
        for k in range(8):
            member = member + jnp.where(routes[:, k:k + 1] == lanes, 1.0, 0.0)
        powers = jnp.where(member > 0.5, jnp.exp(logits), 0.0)
        share = (powers / jnp.sum(powers, axis=1, keepdims=True)).astype(jnp.bfloat16)
        holder = jnp.where(placement[...] == iota((DEVICES, DEVICES), 0), 1.0, 0.0).astype(jnp.bfloat16)
        share = dot_nt(share, holder).astype(jnp.bfloat16)
        for g in range(3):
            weights[g, own(g), :] = share
        for g in range(3):
            for i in (2, 1, 3):
                sp(g, i).start()

    def expand():
        for g, (first, width, axes) in enumerate(GROUPS):
            for i in (1, 2, 3):
                sp(g, i, near(axes[0], -i)).wait_recv()
            total[g][...] = jnp.zeros(total[g].shape, jnp.float32)
            for v in range(SIDE):
                pick = chosen(g, v)
                rank_x[g, :, v * TOK:(v + 1) * TOK] = dot_nt(ranks[g], pick).astype(jnp.bfloat16)
                share_x[g, :, v * TOK:(v + 1) * TOK] = dot_nt(weights[g], pick).astype(jnp.bfloat16)

    for g, (first, width, axes) in enumerate(GROUPS):
        for i in (1, 2, 3):
            sq(g, i, near(axes[0], -i)).wait_recv()
            s1(g, i, near(axes[0], -i)).wait_recv()

    def step(k, carry):
        def stage(lag, run):
            @pl.when(jnp.logical_and(k >= lag, k < lag + ROUNDS))
            def _():
                run(k - lag)

        def once(when, run):
            @pl.when(k == when)
            def _():
                run()

        stage(0, gather)
        once(1, shares)
        stage(1, forward)
        once(2, expand)

        @pl.when(k == 2)
        def _():
            for load in loads:
                load.wait()

        stage(2, expert)
        stage(3, back)
        stage(4, combine)
        return carry

    lax.fori_loop(0, ROUNDS + 4, step, 0)

    for g, (first, width, axes) in enumerate(GROUPS):
        result = total[g][own(g), :]
        for i in (1, 2, 3):
            r1(g, i).wait_recv()
            result = result + back1[g][i - 1].astype(jnp.float32)
        out[:, first:first + width] = result.astype(jnp.bfloat16)

    for i in range(1, 8):
        st(i).wait_send()
    for g in range(3):
        for i in (1, 2, 3):
            sq(g, i).wait_send()
            sp(g, i).wait_send()
            r1(g, i).wait_send()

    def drain(q, carry):
        for g in range(3):
            for i, d in PAIRS:
                if i or d:
                    s3(g, q, i, d).wait_send()
                    r3(g, q, i, d).wait_send()
            for i in (1, 2, 3):
                r2(g, q, i).wait_send()
        return carry

    lax.fori_loop(0, ROUNDS, drain, 0)


def per_group(shape):
    return [pltpu.VMEM(shape(width), jnp.bfloat16) for _, width, _ in GROUPS]


def flat_kernel(*refs):
    args, rest = refs[:9], list(refs[9:])

    def take(n):
        head = rest[:n]
        del rest[:n]
        return head

    blocks = take(3)
    ranks, weights = take(2)
    packed, hop2, arrived, back3, back2, back1, total = (take(3) for _ in range(7))
    kernel(*args, blocks, ranks, weights, packed, hop2, arrived, back3, back2, back1, total, *rest)


def per_device(tokens, norm_gain, router, routes, placement, w_gate, w_up, w_down):
    dma = pltpu.SemaphoreType.DMA
    bf = jnp.bfloat16
    scratch = (
        per_group(lambda w: (SIDE * TOK, w))
        + [pltpu.VMEM((3, SIDE * TOK, DEVICES), bf), pltpu.VMEM((3, SIDE * TOK, DEVICES), bf)]
        + per_group(lambda w: (ROUNDS, 32, 16, w))
        + per_group(lambda w: (ROUNDS, 4, 8, 16, w))
        + per_group(lambda w: (ROUNDS, 8, 4, 16, w))
        + per_group(lambda w: (ROUNDS, 4, 8, 16, w))
        + per_group(lambda w: (ROUNDS, 4, 8, 16, w))
        + per_group(lambda w: (3, TOK, w))
        + [pltpu.VMEM((SIDE * TOK, w), jnp.float32) for _, w, _ in GROUPS]
        + [
            pltpu.VMEM((WIDTH, HIDDEN), bf),
            pltpu.VMEM((WIDTH, HIDDEN), bf),
            pltpu.VMEM((HIDDEN, WIDTH), bf),
            pltpu.VMEM((TOK, WIDTH), bf),
            pltpu.VMEM((WIDTH, DEVICES), bf),
            pltpu.VMEM((SIDE * TOK, WIDTH), bf),
            pltpu.VMEM((SIDE * TOK, HIDDEN), bf),
            pltpu.VMEM((TOK, SIDE * TOK), jnp.float32),
            pltpu.VMEM((3, SIDE * TOK, SIDE * TOK), bf),
            pltpu.VMEM((3, SIDE * TOK, SIDE * TOK), bf),
            dma((3,)),
            dma((8,)), dma((8,)),
            dma((3, 4)), dma((3, 4)),
            dma((3, 4)), dma((3, 4)),
            dma((3, 4)), dma((3, 4)),
            dma((3, ROUNDS, 4)), dma((3, ROUNDS, 4)),
            dma((3, ROUNDS, 8)), dma((3, ROUNDS, 8)),
            dma((3, ROUNDS, 8)), dma((3, ROUNDS, 8)),
            dma((3, ROUNDS, 4)), dma((3, ROUNDS, 4)),
            dma((3, 4)), dma((3, 4)),
        ]
    )
    vmem = pl.BlockSpec(memory_space=pltpu.VMEM)
    whole = pl.BlockSpec(memory_space=pl.ANY)
    return pl.pallas_call(
        flat_kernel,
        name="moe",
        out_shape=jax.ShapeDtypeStruct((TOK, WIDTH), bf),
        in_specs=[vmem] * 5 + [whole] * 3,
        out_specs=vmem,
        scratch_shapes=scratch,
        compiler_params=pltpu.CompilerParams(
            collective_id=0, has_side_effects=True, vmem_limit_bytes=63 * 2**20
        ),
        cost_estimate=pl.CostEstimate(flops=15 * 10**9, bytes_accessed=11 * 10**6, transcendentals=10**6),
    )(tokens, norm_gain.reshape(1, WIDTH), router, routes, placement.reshape(1, DEVICES), w_gate, w_up, w_down)


def solution(mesh):
    placed = (
        P(("rep", "expert"), None),
        P(),
        P("rep", None),
        P(("rep", "expert"), None),
        P(),
        P(("rep", "expert"), None, None),
        P(("rep", "expert"), None, None),
        P(("rep", "expert"), None, None),
    )
    return jax.shard_map(
        per_device,
        mesh=mesh,
        in_specs=placed,
        out_specs=P(("rep", "expert"), None),
        check_vma=False,
    )
```

time: 353 us -> 141 us (0.40); the launches traced: 348 us -> 140 us
  blocking collectives: 232 us -> 0 us
  Pallas kernels: 0 us -> 137 us
  local copies, waits for them, and re-layouts: 75.2 us -> 3.3 us
  matrix products: 21.2 us -> 0 us
  other arithmetic: 13.1 us -> 0 us
  starting transfers between devices: 6.07 us -> 0 us
    pallas_call x0 -> x1, Pallas kernels: none -> 137 us  [per_device(): pl.pallas_call(flat_kernel, name='moe', out_shape=jax.ShapeDtypeStruct((T...]
    all_gather x1 -> x0, blocking collectives: 123 us -> none  [per_device(): lax.all_gather(router, 'rep', axis=0, tiled=True)]
    all_to_all x1 -> x0, blocking collectives: 109 us -> none  [per_device(): lax.all_to_all(outgoing, ('rep', 'expert'), split_axis=0, concat_axis=0,...]
    reshape x4 -> x0, local copies, waits for them, and re-layouts: 42.6 us -> none  [the longest x1 10.7 us: per_device(): collected = returned.reshape(devices * capacity, model_width)[position]]
    dot_general x4 -> x0, matrix products: 21.2 us -> none  [the longest x1 8.2 us: per_device(): gate_proj = jnp.dot(stacked, w_gate[0], preferred_element_type=jnp.float32)]
    gather x6 -> x0, local copies, waits for them, and re-layouts: 19.7 us -> none  [the longest x1 12.6 us: per_device(): collected = returned.reshape(devices * capacity, model_width)[position]]
    scatter x1 -> x0, local copies, waits for them, and re-layouts: 10.7 us -> none  [per_device(): jnp.zeros((devices * capacity, model_width), jnp.bfloat16).at[position]]
    reduce_sum x4 -> x0, other arithmetic: 9.74 us -> none  [the longest x1 7.32 us: per_device(): jnp.sum(weighted.reshape(tok_rows, top_count, model_width), axis=1)]
  transfers between devices with their start and end apart: 1 -> 0, of which waited for: 0 -> 0; matrix products, arithmetic and copies ran while one was open for 2% -> 0% of each run, Pallas kernels for 0% -> 0%
where the time goes in v1:
time: 141 us; the launch traced here: 140 us
  Pallas kernels  137 us (97%)
  local copies, waits for them, and re-layouts  3.3 us (2%)
    pallas_call x1, Pallas kernels, per_device(): pl.pallas_call(flat_kernel, name='moe', out_shape=jax.ShapeDtypeStruct((T...  137 us
    unnamed x2, local copies, waits for them, and re-layouts  3.3 us

profile of v1, /device:TPU:0, one launch (start us, length us, event | category | flops | bytes accessed | tf_op | source)
XLA Modules:
  0.0 140.3 jit_solution(7813029255352279463)
XLA Ops:
  0.0 1.4 %copy.9.refs_3_ = s32[128,8]{1,0:T(8,128)} copy(s32[128,8]{0,1:T(8,128)} %param.11) | data formatting | bytes 8192 | tf_op args[3]
  1.4 137.0 %moe.1 = bf16[128,2048]{1,0:T(8,128)(2,1)} custom-call(bf16[128,2048]{1,0:T(8,128)(2,1)} %refs_0_.1, f32[1,2048]{1,0:T(1,128)} %bitcast.2, bf16[256,128]{1,0:T(8,128)(2,1)} %refs_2_.1, s32[128,8]{1,0:T(8,128)} %copy.9.refs_3_, s32[1,128]{1,0:T(1,128)} %bitcast.3, bf16[1,2048,768]{2,1,0:T(8,128)(2,1)} %refs_5_.1, bf16[1,2048,768]{2,1,0:T(8,128)(2,1)} %refs_6_.1, ...), custom_call_target="tpu_custom_call" | custom-call | flops 15000000512 | bytes 11000000 | tf_op jit(solution)/shard_map/moe/pallas_call | solution.py:439
  138.4 1.9 %copy.11 = bf16[128,2048]{1,0:T(8,128)(2,1)} copy(bf16[128,2048]{1,0:T(8,128)(2,1)} %moe.1) | data formatting | bytes 1048576

commit v2 on v1

--- a/solution.py
+++ b/solution.py
@@ -14,11 +14,13 @@
 SLOTS = 4
 DEVICES = 128
 GROUPS = (
-    (0, 768, (0, 1, 2)),
-    (768, 640, (1, 2, 0)),
-    (1408, 640, (2, 0, 1)),
+    (0, 768, (2, 0, 1)),
+    (768, 640, (0, 1, 2)),
+    (1408, 640, (1, 2, 0)),
 )
 NT = (((1,), (1,)), ((), ()))
+TN = (((0,), (0,)), ((), ()))
+PIECE = 32
 
 
 def iota(shape, dim):
@@ -31,14 +33,19 @@
 
 def dot_nt(a, b):
     return lax.dot_general(a, b, NT, preferred_element_type=jnp.float32)
+
+
+def dot_tn(a, b):
+    return lax.dot_general(a, b, TN, preferred_element_type=jnp.float32)
 
 
 def kernel(
     tokens, gain, router, routes, placement, w_gate, w_up, w_down, out,
     blocks, ranks, weights, packed, hop2, arrived, back3, back2, back1, total,
-    gate_v, up_v, down_v, normed, table, stacked, hidden, slot_of, rank_x, share_x,
-    w_sem, t_send, t_recv, s1_send, s1_recv, q_send, q_recv, p_send, p_recv,
-    s2_send, s2_recv, s3_send, s3_recv, r3_send, r3_recv, r2_send, r2_recv, r1_send, r1_recv,
+    gate_v, up_v, down_v, normed, table, pieces, stacked, hidden, slot_of, mix,
+    tokens_v, gain_v, routes_v, placement_v, ranks_out, shares_out,
+    w_sem, in_sem, out_sem, t_send, t_recv, u_send, u_recv,
+    s1_send, s1_recv, q_send, q_recv, p_send, p_recv, s2_send, s2_recv, s3_send, s3_recv, r3_send, r3_recv, r2_send, r2_recv, r1_send, r1_recv,
 ):
     rep = lax.axis_index("rep")
     exp = lax.axis_index("expert")
@@ -63,6 +70,24 @@
             device_id=dev, device_id_type=MESH,
         )
 
+    barrier = pltpu.get_barrier_semaphore()
+    greeted = [along(a, near(a, i), (core + d) % 2) for a in range(3) for i in (1, 2, 3) for d in (0, 1)]
+    greeted.append(device(at, 1 - core))
+    greeted += [device((near(0, i), near(1, 2), at[2]), core) for i in (1, 2, 3)]
+    for dev in greeted:
+        pl.semaphore_signal(barrier, inc=1, device_id=dev, device_id_type=MESH)
+
+    mine = core * 4 + at[2]
+    operands = [
+        pltpu.make_async_copy(tokens, tokens_v, in_sem.at[0]),
+        pltpu.make_async_copy(gain, gain_v, in_sem.at[1]),
+        pltpu.make_async_copy(routes, routes_v, in_sem.at[2]),
+        pltpu.make_async_copy(placement, placement_v, in_sem.at[3]),
+        pltpu.make_async_copy(
+            router.at[pl.ds(pl.multiple_of(mine * PIECE, PIECE), PIECE)], pieces.at[mine, rep], in_sem.at[4]),
+    ]
+    for load in operands:
+        load.start()
     loads = [
         pltpu.make_async_copy(w_gate.at[0], gate_v, w_sem.at[0]),
         pltpu.make_async_copy(w_up.at[0], up_v, w_sem.at[1]),
@@ -71,30 +96,41 @@
     for load in loads:
         load.start()
 
-    barrier = pltpu.get_barrier_semaphore()
-    greeted = [along(a, near(a, i), (core + d) % 2) for a in range(3) for i in (1, 2, 3) for d in (0, 1)]
-    greeted.append(device(at, 1 - core))
-    greeted += [device((near(0, i), near(1, 2), at[2]), core) for i in (1, 2, 3)]
-    for dev in greeted:
-        pl.semaphore_signal(barrier, inc=1, device_id=dev, device_id_type=MESH)
-
-    values = tokens[...].astype(jnp.float32)
+    operands[0].wait()
+    operands[1].wait()
+    values = tokens_v[...].astype(jnp.float32)
     scale = lax.rsqrt(jnp.mean(values * values, axis=-1, keepdims=True) + 1e-06)
-    normed[...] = (values * scale * gain[...]).astype(jnp.bfloat16)
+    normed[...] = (values * scale * gain_v[...]).astype(jnp.bfloat16)
     for g, (first, width, axes) in enumerate(GROUPS):
         blocks[g][pl.ds(pl.multiple_of(at[axes[0]] * TOK, TOK), TOK), :] = normed[:, first:first + width]
 
-    member = jnp.zeros((TOK, DEVICES), jnp.float32)
-    lanes = iota((TOK, DEVICES), 1)
-    for k in range(8):
-        member = member + jnp.where(routes[:, k:k + 1] == lanes, 1.0, 0.0)
-    holder = jnp.where(placement[...] == iota((DEVICES, DEVICES), 0), 1.0, 0.0).astype(jnp.bfloat16)
-    by_slot = dot_nt(member.astype(jnp.bfloat16), holder)
-    before = jnp.where(iota((TOK, TOK), 1) < iota((TOK, TOK), 0), 1.0, 0.0).astype(jnp.bfloat16)
-    rank = jnp.where(by_slot > 0.5, dot(before, by_slot.astype(jnp.bfloat16)), -1.0).astype(jnp.bfloat16)
+    def holder(g):
+        a1, a2, a3 = GROUPS[g][2]
+        r = iota((DEVICES, DEVICES), 0)
+        pos = [None, None, None]
+        pos[a1] = r // 32
+        pos[a2] = (r // 8) % 4
+        pos[a3] = (r // 2) % 4
+        wanted = pos[0] * 32 + pos[1] * 8 + pos[2] * 2 + r % 2
+        return jnp.where(placement_v[...] == wanted, 1.0, 0.0).astype(jnp.bfloat16)
+
+    def members():
+        found = jnp.zeros((DEVICES, TOK), jnp.float32)
+        rows = iota((DEVICES, TOK), 0)
+        for k in range(8):
+            found = found + jnp.where(routes_v[k:k + 1, :] == rows, 1.0, 0.0)
+        return found
+
+    operands[2].wait()
+    operands[3].wait()
+    member = members()
+    before = jnp.where(iota((TOK, TOK), 0) < iota((TOK, TOK), 1), 1.0, 0.0).astype(jnp.bfloat16)
+    rank = jnp.where(member > 0.5, dot(member.astype(jnp.bfloat16), before), -1.0).astype(jnp.bfloat16)
     for g, (first, width, axes) in enumerate(GROUPS):
-        ranks[g, pl.ds(pl.multiple_of(at[axes[0]] * TOK, TOK), TOK), :] = rank
-    table[pl.ds(pl.multiple_of(rep * 256, 256), 256), :] = router[...]
+        ranks_out[g] = dot(holder(g), rank).astype(jnp.bfloat16)
+        ranks[g, :, pl.ds(pl.multiple_of(at[axes[0]] * TOK, TOK), TOK)] = ranks_out[
+            g, pl.ds(pl.multiple_of(at[axes[0]] * 32, 32), 32), :]
+    operands[4].wait()
 
     pl.semaphore_wait(barrier, len(greeted))
 
@@ -107,28 +143,41 @@
         return remote(blocks[g].at[own(g)], blocks[g].at[own(g, where)], s1_send.at[g, i], s1_recv.at[g, i],
                       along(a, near(a, i), core))
 
+    def lane(g, where=None):
+        position = at[GROUPS[g][2][0]] if where is None else where
+        return pl.ds(pl.multiple_of(position * TOK, TOK), TOK)
+
     def sq(g, i, where=None):
         a = GROUPS[g][2][0]
-        return remote(ranks.at[g, own(g)], ranks.at[g, own(g, where)], q_send.at[g, i], q_recv.at[g, i],
-                      along(a, near(a, i), core))
+        v = near(a, i)
+        return remote(ranks_out.at[g, pl.ds(pl.multiple_of(v * 32, 32), 32)], ranks.at[g, :, lane(g, where)],
+                      q_send.at[g, i], q_recv.at[g, i], along(a, v, core))
 
     def sp(g, i, where=None):
         a = GROUPS[g][2][0]
-        return remote(weights.at[g, own(g)], weights.at[g, own(g, where)], p_send.at[g, i], p_recv.at[g, i],
-                      along(a, near(a, i), core))
-
-    def shard(r):
-        return table.at[pl.ds(pl.multiple_of(r * 256, 256), 256)]
+        v = near(a, i)
+        return remote(shares_out.at[g, pl.ds(pl.multiple_of(v * 32, 32), 32)], weights.at[g, :, lane(g, where)],
+                      p_send.at[g, i], p_recv.at[g, i], along(a, v, core))
 
     def st(i, r=None):
-        return remote(shard(rep), shard(rep if r is None else r), t_send.at[i], t_recv.at[i], ((rep + i) % 8, exp))
-
+        return remote(pieces.at[mine, rep], pieces.at[mine, rep if r is None else r],
+                      t_send.at[i], t_recv.at[i], ((rep + i) % 8, exp))
+
+    def su(i, where=None):
+        return remote(pieces.at[mine], pieces.at[mine if where is None else core * 4 + where],
+                      u_send.at[i], u_recv.at[i], along(2, near(2, i), core))
+
+    def sv(c=None):
+        here = core if c is None else c
+        return remote(pieces.at[pl.ds(core * 4, 4)], pieces.at[pl.ds(here * 4, 4)],
+                      u_send.at[0], u_recv.at[0], device(at, 1 - core))
+
+    for i in (2, 1, 3):
+        for g in range(3):
+            s1(g, i).start()
     for g in range(3):
         for i in (2, 1, 3):
             sq(g, i).start()
-    for i in (2, 1, 3):
-        for g in range(3):
-            s1(g, i).start()
     for i in range(1, 8):
         st(i).start()
 
@@ -136,22 +185,16 @@
     col = iota((TOK, SIDE * TOK), 1)
     slot_of[...] = jnp.where((row // 4) % 4 == col // TOK, row % 4, 1000).astype(jnp.float32)
 
-    def chosen(g, v):
-        a1, a2, a3 = GROUPS[g][2]
-        r = iota((TOK, DEVICES), 0)
-        s = iota((TOK, DEVICES), 1)
-        pos = [None, None, None]
-        pos[a1] = at[a1]
-        pos[a2] = v
-        pos[a3] = r // 32
-        wanted = pos[0] * 32 + pos[1] * 8 + pos[2] * 2 + (r // 16) % 2
-        return jnp.where(s == wanted, 1.0, 0.0).astype(jnp.bfloat16)
+    def spread(v, plane):
+        r = iota((TOK, 32), 0)
+        pick = jnp.where(iota((TOK, 32), 1) == v * 8 + r // 16, 1.0, 0.0).astype(jnp.bfloat16)
+        return dot(pick, plane)
 
     def swap(g):
         r = iota((256, 256), 0)
         c = iota((256, 256), 1)
         a, b, d, s = r // 64, (r // 16) % 4, (r // 4) % 4, r % 4
-        if g == 0:
+        if GROUPS[g][2][0] == 0:
             wanted = d * 64 + b * 16 + a * 4 + s
         else:
             wanted = a * 64 + d * 16 + b * 4 + s
@@ -201,7 +244,7 @@
         for i in (2, 1, 3, 0):
             for g, (first, width, axes) in enumerate(GROUPS):
                 v = near(axes[1], i)
-                found = dot_nt(chosen(g, v), ranks[g])
+                found = spread(v, ranks[g])
                 pick = jnp.where(found == slot, 1.0, 0.0).astype(jnp.bfloat16)
                 rows = dot(pick, blocks[g][...]).astype(jnp.bfloat16).reshape(8, 16, width)
                 if i == 0:
@@ -227,7 +270,7 @@
                     copy.wait_recv()
             for c in (0, 1):
                 part = arrived[g][q, pl.ds(c * 4, 4)]
-                if g == 2:
+                if axes[0] == 2:
                     for y in range(4):
                         for z in range(4):
                             at_row = c * 256 + z * 64 + y * 16
@@ -250,7 +293,7 @@
                 s2(g, q, i).wait_send()
             for c in (0, 1):
                 half = result[c * 256:(c + 1) * 256]
-                if g == 2:
+                if axes[0] == 2:
                     half = half.reshape(4, 4, 16, width)
                     for y in range(4):
                         for z in range(4):
@@ -276,12 +319,11 @@
             for i in (1, 2, 3):
                 r2(g, q, i, near(axes[1], -i)).wait_recv()
             r2(g, q, 0).wait()
-            slot = (q * SLOTS).astype(jnp.float32)
-            r = iota((SIDE * TOK, SIDE * TOK), 0)
-            s = iota((SIDE * TOK, SIDE * TOK), 1)
-            wanted = jnp.where((s // 4) % 4 == r // TOK, s % 4, 1000).astype(jnp.float32) + slot
-            mix = jnp.where(rank_x[g].astype(jnp.float32) == wanted, share_x[g].astype(jnp.float32), 0.0)
-            total[g][...] += dot(mix.astype(jnp.bfloat16), back2[g][q].reshape(SIDE * TOK, width))
+            slot = slot_of[...] + (q * SLOTS).astype(jnp.float32)
+            for v in range(SIDE):
+                mix[v * TOK:(v + 1) * TOK, :] = jnp.where(
+                    spread(v, ranks[g]) == slot, spread(v, weights[g]), 0.0).astype(jnp.bfloat16)
+            total[g][...] += dot_tn(mix[...], back2[g][q].reshape(SIDE * TOK, width))
 
             @pl.when(q == ROUNDS - 1)
             def _():
@@ -291,33 +333,39 @@
                 for i in (2, 1, 3):
                     r1(g, i).start()
 
-    def shares():
+    def along_x():
         for i in range(1, 8):
             st(i, (rep + 8 - i) % 8).wait_recv()
+        for i in (2, 1, 3):
+            su(i).start()
+
+    def across():
+        for i in (1, 2, 3):
+            su(i, near(2, -i)).wait_recv()
+        sv().start()
+
+    def shares():
+        sv(1 - core).wait_recv()
+        for r in range(8):
+            for p in range(8):
+                table[r * 256 + p * PIECE:r * 256 + (p + 1) * PIECE, :] = pieces[p, r]
         logits = dot(normed[...], table[...])
-        member = jnp.zeros((TOK, DEVICES), jnp.float32)
-        lanes = iota((TOK, DEVICES), 1)
-        for k in range(8):
-            member = member + jnp.where(routes[:, k:k + 1] == lanes, 1.0, 0.0)
+        eye = jnp.where(iota((TOK, TOK), 0) == iota((TOK, TOK), 1), 1.0, 0.0).astype(jnp.bfloat16)
+        member = dot_nt(eye, members().astype(jnp.bfloat16))
         powers = jnp.where(member > 0.5, jnp.exp(logits), 0.0)
         share = (powers / jnp.sum(powers, axis=1, keepdims=True)).astype(jnp.bfloat16)
-        holder = jnp.where(placement[...] == iota((DEVICES, DEVICES), 0), 1.0, 0.0).astype(jnp.bfloat16)
-        share = dot_nt(share, holder).astype(jnp.bfloat16)
-        for g in range(3):
-            weights[g, own(g), :] = share
+        for g, (first, width, axes) in enumerate(GROUPS):
+            shares_out[g] = dot_nt(holder(g), share).astype(jnp.bfloat16)
+            weights[g, :, lane(g)] = shares_out[g, pl.ds(pl.multiple_of(at[axes[0]] * 32, 32), 32), :]
         for g in range(3):
             for i in (2, 1, 3):
                 sp(g, i).start()
 
-    def expand():
+    def prepare():
         for g, (first, width, axes) in enumerate(GROUPS):
             for i in (1, 2, 3):
                 sp(g, i, near(axes[0], -i)).wait_recv()
             total[g][...] = jnp.zeros(total[g].shape, jnp.float32)
-            for v in range(SIDE):
-                pick = chosen(g, v)
-                rank_x[g, :, v * TOK:(v + 1) * TOK] = dot_nt(ranks[g], pick).astype(jnp.bfloat16)
-                share_x[g, :, v * TOK:(v + 1) * TOK] = dot_nt(weights[g], pick).astype(jnp.bfloat16)
 
     for g, (first, width, axes) in enumerate(GROUPS):
         for i in (1, 2, 3):
@@ -336,9 +384,10 @@
                 run()
 
         stage(0, gather)
-        once(1, shares)
+        once(0, along_x)
+        once(1, across)
         stage(1, forward)
-        once(2, expand)
+        once(2, shares)
 
         @pl.when(k == 2)
         def _():
@@ -347,18 +396,27 @@
 
         stage(2, expert)
         stage(3, back)
+        once(3, prepare)
         stage(4, combine)
         return carry
 
     lax.fori_loop(0, ROUNDS + 4, step, 0)
+
+    def leave(g):
+        first, width, axes = GROUPS[g]
+        return pltpu.make_async_copy(
+            normed.at[:, first:first + width], out.at[:, first:first + width], out_sem.at[g])
 
     for g, (first, width, axes) in enumerate(GROUPS):
         result = total[g][own(g), :]
         for i in (1, 2, 3):
             r1(g, i).wait_recv()
             result = result + back1[g][i - 1].astype(jnp.float32)
-        out[:, first:first + width] = result.astype(jnp.bfloat16)
-
+        normed[:, first:first + width] = result.astype(jnp.bfloat16)
+        leave(g).start()
+
+    for i in (0, 1, 2, 3):
+        (su(i) if i else sv()).wait_send()
     for i in range(1, 8):
         st(i).wait_send()
     for g in range(3):
@@ -378,6 +436,8 @@
         return carry
 
     lax.fori_loop(0, ROUNDS, drain, 0)
+    for g in range(3):
+        leave(g).wait()
 
 
 def per_group(shape):
@@ -403,7 +463,7 @@
     bf = jnp.bfloat16
     scratch = (
         per_group(lambda w: (SIDE * TOK, w))
-        + [pltpu.VMEM((3, SIDE * TOK, DEVICES), bf), pltpu.VMEM((3, SIDE * TOK, DEVICES), bf)]
+        + [pltpu.VMEM((3, 32, SIDE * TOK), bf), pltpu.VMEM((3, 32, SIDE * TOK), bf)]
         + per_group(lambda w: (ROUNDS, 32, 16, w))
         + per_group(lambda w: (ROUNDS, 4, 8, 16, w))
         + per_group(lambda w: (ROUNDS, 8, 4, 16, w))
@@ -417,13 +477,20 @@
             pltpu.VMEM((HIDDEN, WIDTH), bf),
             pltpu.VMEM((TOK, WIDTH), bf),
             pltpu.VMEM((WIDTH, DEVICES), bf),
+            pltpu.VMEM((8, 8, PIECE, DEVICES), bf),
             pltpu.VMEM((SIDE * TOK, WIDTH), bf),
             pltpu.VMEM((SIDE * TOK, HIDDEN), bf),
             pltpu.VMEM((TOK, SIDE * TOK), jnp.float32),
-            pltpu.VMEM((3, SIDE * TOK, SIDE * TOK), bf),
-            pltpu.VMEM((3, SIDE * TOK, SIDE * TOK), bf),
-            dma((3,)),
+            pltpu.VMEM((SIDE * TOK, SIDE * TOK), bf),
+            pltpu.VMEM((TOK, WIDTH), bf),
+            pltpu.VMEM((1, WIDTH), jnp.float32),
+            pltpu.VMEM((8, TOK), jnp.int32),
+            pltpu.VMEM((1, DEVICES), jnp.int32),
+            pltpu.VMEM((3, DEVICES, TOK), bf),
+            pltpu.VMEM((3, DEVICES, TOK), bf),
+            dma((3,)), dma((5,)), dma((3,)),
             dma((8,)), dma((8,)),
+            dma((4,)), dma((4,)),
             dma((3, 4)), dma((3, 4)),
             dma((3, 4)), dma((3, 4)),
             dma((3, 4)), dma((3, 4)),
@@ -434,20 +501,19 @@
             dma((3, 4)), dma((3, 4)),
         ]
     )
-    vmem = pl.BlockSpec(memory_space=pltpu.VMEM)
     whole = pl.BlockSpec(memory_space=pl.ANY)
     return pl.pallas_call(
         flat_kernel,
         name="moe",
         out_shape=jax.ShapeDtypeStruct((TOK, WIDTH), bf),
-        in_specs=[vmem] * 5 + [whole] * 3,
-        out_specs=vmem,
+        in_specs=[whole] * 8,
+        out_specs=whole,
         scratch_shapes=scratch,
         compiler_params=pltpu.CompilerParams(
             collective_id=0, has_side_effects=True, vmem_limit_bytes=63 * 2**20
         ),
         cost_estimate=pl.CostEstimate(flops=15 * 10**9, bytes_accessed=11 * 10**6, transcendentals=10**6),
-    )(tokens, norm_gain.reshape(1, WIDTH), router, routes, placement.reshape(1, DEVICES), w_gate, w_up, w_down)
+    )(tokens, norm_gain.reshape(1, WIDTH), router, routes.T, placement.reshape(1, DEVICES), w_gate, w_up, w_down)
 
 
 def solution(mesh):

time: 141 us -> 136 us (0.965)
  Pallas kernels: 137 us -> 133 us
  local copies, waits for them, and re-layouts: 3.3 us -> 1.88 us
    pallas_call x1, Pallas kernels: 137 us -> 133 us  [per_device(): pl.pallas_call(flat_kernel, name='moe', out_shape=jax.ShapeDtypeStruct((T...]
    unnamed x2 -> x1, local copies, waits for them, and re-layouts: 3.3 us -> 1.88 us
where the time goes in v2:
time: 136 us; the launch traced here: 135 us
  Pallas kernels  133 us (98%)
  local copies, waits for them, and re-layouts  1.88 us (1%)
    pallas_call x1, Pallas kernels, per_device(): pl.pallas_call(flat_kernel, name='moe', out_shape=jax.ShapeDtypeStruct((T...  133 us

profile of v2, /device:TPU:0, one launch (start us, length us, event | category | flops | bytes accessed | tf_op | source)
XLA Modules:
  0.0 134.8 jit_solution(7175877002513122788)
XLA Ops:
  0.0 132.9 %moe.1 = bf16[128,2048]{1,0:T(8,128)(2,1)} custom-call(bf16[128,2048]{1,0:T(8,128)(2,1)} %refs_0_.1, f32[1,2048]{1,0:T(1,128)} %bitcast.3, bf16[256,128]{1,0:T(8,128)(2,1)} %refs_2_.1, s32[8,128]{1,0:T(8,128)} %bitcast.4, s32[1,128]{1,0:T(1,128)} %bitcast.5, bf16[1,2048,768]{2,1,0:T(8,128)(2,1)} %refs_5_.1, bf16[1,2048,768]{2,1,0:T(8,128)(2,1)} %refs_6_.1, ...), custom_call_target="tpu_custom_call" | custom-call | flops 15000000512 | bytes 11000000 | tf_op jit(solution)/shard_map/moe/pallas_call | solution.py:505
  132.9 1.9 %copy.10 = bf16[128,2048]{1,0:T(8,128)(2,1)} copy(bf16[128,2048]{1,0:T(8,128)(2,1)} %moe.1) | data formatting | bytes 1048576

commit v3 on v2

--- a/solution.py
+++ b/solution.py
@@ -40,8 +40,8 @@
 
 
 def kernel(
-    tokens, gain, router, routes, placement, w_gate, w_up, w_down, out,
-    blocks, ranks, weights, packed, hop2, arrived, back3, back2, back1, total,
+    tokens, gain, router, routes, placement, w_gate, w_up, w_down, own_out, parts,
+    blocks, ranks, weights, packed, hop2, arrived, back3, back2, total,
     gate_v, up_v, down_v, normed, table, pieces, stacked, hidden, slot_of, mix,
     tokens_v, gain_v, routes_v, placement_v, ranks_out, shares_out,
     w_sem, in_sem, out_sem, t_send, t_recv, u_send, u_recv,
@@ -69,6 +69,12 @@
             src_ref=src, dst_ref=dst, send_sem=send, recv_sem=recv,
             device_id=dev, device_id_type=MESH,
         )
+
+    def came(ref, sem):
+        remote(ref, ref, sem, sem, device(at, 1 - core)).wait_recv()
+
+    def went(ref, sem):
+        remote(ref, ref, sem, sem, device(at, 1 - core)).wait_send()
 
     barrier = pltpu.get_barrier_semaphore()
     greeted = [along(a, near(a, i), (core + d) % 2) for a in range(3) for i in (1, 2, 3) for d in (0, 1)]
@@ -134,42 +140,39 @@
 
     pl.semaphore_wait(barrier, len(greeted))
 
-    def own(g, where=None):
-        position = at[GROUPS[g][2][0]] if where is None else where
+    def block(g, position):
         return pl.ds(pl.multiple_of(position * TOK, TOK), TOK)
 
-    def s1(g, i, where=None):
+    def own(g):
+        return block(g, at[GROUPS[g][2][0]])
+
+    def s1(g, i):
         a = GROUPS[g][2][0]
-        return remote(blocks[g].at[own(g)], blocks[g].at[own(g, where)], s1_send.at[g, i], s1_recv.at[g, i],
+        return remote(blocks[g].at[own(g)], blocks[g].at[own(g)], s1_send.at[g], s1_recv.at[g],
                       along(a, near(a, i), core))
 
-    def lane(g, where=None):
-        position = at[GROUPS[g][2][0]] if where is None else where
-        return pl.ds(pl.multiple_of(position * TOK, TOK), TOK)
-
-    def sq(g, i, where=None):
+    def sq(g, i):
         a = GROUPS[g][2][0]
         v = near(a, i)
-        return remote(ranks_out.at[g, pl.ds(pl.multiple_of(v * 32, 32), 32)], ranks.at[g, :, lane(g, where)],
-                      q_send.at[g, i], q_recv.at[g, i], along(a, v, core))
-
-    def sp(g, i, where=None):
+        return remote(ranks_out.at[g, pl.ds(pl.multiple_of(v * 32, 32), 32)], ranks.at[g, :, own(g)],
+                      q_send.at[0], q_recv.at[0], along(a, v, core))
+
+    def sp(g, i):
         a = GROUPS[g][2][0]
         v = near(a, i)
-        return remote(shares_out.at[g, pl.ds(pl.multiple_of(v * 32, 32), 32)], weights.at[g, :, lane(g, where)],
-                      p_send.at[g, i], p_recv.at[g, i], along(a, v, core))
-
-    def st(i, r=None):
-        return remote(pieces.at[mine, rep], pieces.at[mine, rep if r is None else r],
-                      t_send.at[i], t_recv.at[i], ((rep + i) % 8, exp))
-
-    def su(i, where=None):
-        return remote(pieces.at[mine], pieces.at[mine if where is None else core * 4 + where],
-                      u_send.at[i], u_recv.at[i], along(2, near(2, i), core))
-
-    def sv(c=None):
-        here = core if c is None else c
-        return remote(pieces.at[pl.ds(core * 4, 4)], pieces.at[pl.ds(here * 4, 4)],
+        return remote(shares_out.at[g, pl.ds(pl.multiple_of(v * 32, 32), 32)], weights.at[g, :, own(g)],
+                      p_send.at[0], p_recv.at[0], along(a, v, core))
+
+    def st(i):
+        return remote(pieces.at[mine, rep], pieces.at[mine, rep],
+                      t_send.at[0], t_recv.at[0], ((rep + i) % 8, exp))
+
+    def su(i):
+        return remote(pieces.at[mine], pieces.at[mine],
+                      u_send.at[1], u_recv.at[1], along(2, near(2, i), core))
+
+    def sv():
+        return remote(pieces.at[pl.ds(core * 4, 4)], pieces.at[pl.ds(core * 4, 4)],
                       u_send.at[0], u_recv.at[0], device(at, 1 - core))
 
     for i in (2, 1, 3):
@@ -200,41 +203,42 @@
             wanted = a * 64 + d * 16 + b * 4 + s
         return jnp.where(c == wanted, 1.0, 0.0).astype(jnp.bfloat16)
 
-    def s2(g, q, i, where=None):
+    def s2(g, q, i):
         a = GROUPS[g][2][1]
         v = near(a, i)
-        return remote(packed[g].at[q, pl.ds(v * 8, 8)], hop2[g].at[q, at[a] if where is None else where],
-                      s2_send.at[g, q, i], s2_recv.at[g, q, i], along(a, v, core))
-
-    def s3(g, q, i, d, where=None):
+        return remote(packed[g].at[q, pl.ds(v * 8, 8)], hop2[g].at[q, at[a]],
+                      s2_send.at[g, q], s2_recv.at[g, q], along(a, v, core))
+
+    def s3(g, q, i, d):
         a = GROUPS[g][2][2]
         u, c = near(a, i), (core + d) % 2
         src = hop2[g].at[q, :, u * 2 + c]
-        dst = arrived[g].at[q, core * 4 + at[a] if where is None else where]
+        dst = arrived[g].at[q, core * 4 + at[a]]
         if i == 0 and d == 0:
-            return pltpu.make_async_copy(src, dst, s3_recv.at[g, q, 0])
-        return remote(src, dst, s3_send.at[g, q, i * 2 + d], s3_recv.at[g, q, i * 2 + d], along(a, u, c))
-
-    def r3(g, q, i, d, where=None):
+            return pltpu.make_async_copy(src, dst, s3_recv.at[g, q])
+        return remote(src, dst, s3_send.at[g], s3_recv.at[g, q], along(a, u, c))
+
+    def r3(g, q, i, d):
         a = GROUPS[g][2][2]
         u, c = near(a, i), (core + d) % 2
         src = packed[g].at[q, pl.ds((c * 4 + u) * 4, 4)]
-        dst = back3[g].at[q, :, at[a] * 2 + core if where is None else where]
+        dst = back3[g].at[q, :, at[a] * 2 + core]
         if i == 0 and d == 0:
-            return pltpu.make_async_copy(src, dst, r3_recv.at[g, q, 0])
-        return remote(src, dst, r3_send.at[g, q, i * 2 + d], r3_recv.at[g, q, i * 2 + d], along(a, u, c))
-
-    def r2(g, q, i, where=None):
+            return pltpu.make_async_copy(src, dst, r3_recv.at[g, q])
+        return remote(src, dst, r3_send.at[g], r3_recv.at[g, q], along(a, u, c))
+
+    def r2(g, q, i):
         a = GROUPS[g][2][1]
         v = near(a, i)
-        src, dst = back3[g].at[q, v], back2[g].at[q, at[a] if where is None else where]
+        src, dst = back3[g].at[q, v], back2[g].at[q, at[a]]
         if i == 0:
-            return pltpu.make_async_copy(src, dst, r2_recv.at[g, q, 0])
-        return remote(src, dst, r2_send.at[g, q, i], r2_recv.at[g, q, i], along(a, v, core))
+            return pltpu.make_async_copy(src, dst, r2_recv.at[g, q])
+        return remote(src, dst, r2_send.at[g], r2_recv.at[g, q], along(a, v, core))
 
     def r1(g, i):
-        a = GROUPS[g][2][0]
-        return remote(blocks[g].at[own(g, near(a, i))], back1[g].at[i - 1], r1_send.at[g, i], r1_recv.at[g, i],
+        first, width, axes = GROUPS[g]
+        a = axes[0]
+        return remote(blocks[g].at[block(g, near(a, i))], parts.at[i - 1, :, first:first + width], r1_send.at[g], r1_recv.at[g],
                       along(a, near(a, i), core))
 
     PAIRS = [(i, d) for i in (2, 1, 3, 0) for d in (0, 1)]
@@ -255,19 +259,13 @@
 
     def forward(q):
         for g in range(3):
-            for i in (1, 2, 3):
-                s2(g, q, i, near(GROUPS[g][2][1], -i)).wait_recv()
+            came(hop2[g].at[q, pl.ds(0, 3)], s2_recv.at[g, q])
             for i, d in PAIRS:
                 s3(g, q, i, d).start()
 
     def expert(q):
         for g, (first, width, axes) in enumerate(GROUPS):
-            for i, d in PAIRS:
-                copy = s3(g, q, i, d, ((core + d) % 2) * 4 + near(axes[2], -i))
-                if i == 0 and d == 0:
-                    copy.wait()
-                else:
-                    copy.wait_recv()
+            came(arrived[g].at[q], s3_recv.at[g, q])
             for c in (0, 1):
                 part = arrived[g][q, pl.ds(c * 4, 4)]
                 if axes[0] == 2:
@@ -289,8 +287,7 @@
         lax.fori_loop(0, HIDDEN // 256, tile, 0)
         for g, (first, width, axes) in enumerate(GROUPS):
             result = dot(hidden[...], down_v[:, first:first + width]).astype(jnp.bfloat16)
-            for i in (1, 2, 3):
-                s2(g, q, i).wait_send()
+            went(packed[g].at[q, pl.ds(0, 24)], s2_send.at[g, q])
             for c in (0, 1):
                 half = result[c * 256:(c + 1) * 256]
                 if axes[0] == 2:
@@ -305,47 +302,44 @@
 
     def back(q):
         for g, (first, width, axes) in enumerate(GROUPS):
-            for i, d in PAIRS:
-                copy = r3(g, q, i, d, near(axes[2], -i) * 2 + (core + d) % 2)
-                if i == 0 and d == 0:
-                    copy.wait()
-                else:
-                    copy.wait_recv()
+            came(back3[g].at[q], r3_recv.at[g, q])
             for i in (2, 1, 3, 0):
                 r2(g, q, i).start()
 
+    def leave(g):
+        first, width, axes = GROUPS[g]
+        return pltpu.make_async_copy(
+            total[g].at[own(g)], own_out.at[:, first:first + width], out_sem.at[g])
+
     def combine(q):
+        slot = slot_of[...] + (q * SLOTS).astype(jnp.float32)
+        for g in range(3):
+            for v in range(SIDE):
+                mix[g, v * TOK:(v + 1) * TOK, :] = jnp.where(
+                    spread(v, ranks[g]) == slot, spread(v, weights[g]), 0.0).astype(jnp.bfloat16)
         for g, (first, width, axes) in enumerate(GROUPS):
-            for i in (1, 2, 3):
-                r2(g, q, i, near(axes[1], -i)).wait_recv()
-            r2(g, q, 0).wait()
-            slot = slot_of[...] + (q * SLOTS).astype(jnp.float32)
-            for v in range(SIDE):
-                mix[v * TOK:(v + 1) * TOK, :] = jnp.where(
-                    spread(v, ranks[g]) == slot, spread(v, weights[g]), 0.0).astype(jnp.bfloat16)
-            total[g][...] += dot_tn(mix[...], back2[g][q].reshape(SIDE * TOK, width))
+            came(back2[g].at[q], r2_recv.at[g, q])
+            total[g][...] += dot_tn(mix[g], back2[g][q].reshape(SIDE * TOK, width))
 
             @pl.when(q == ROUNDS - 1)
             def _():
-                for i in (1, 2, 3):
-                    s1(g, i).wait_send()
+                went(blocks[g].at[pl.ds(0, 3 * TOK)], s1_send.at[g])
                 blocks[g][...] = total[g][...].astype(jnp.bfloat16)
                 for i in (2, 1, 3):
                     r1(g, i).start()
+                leave(g).start()
 
     def along_x():
-        for i in range(1, 8):
-            st(i, (rep + 8 - i) % 8).wait_recv()
+        came(pieces.at[mine, pl.ds(0, 7)], t_recv.at[0])
         for i in (2, 1, 3):
             su(i).start()
 
     def across():
-        for i in (1, 2, 3):
-            su(i, near(2, -i)).wait_recv()
+        came(pieces.at[pl.ds(0, 3)], u_recv.at[1])
         sv().start()
 
     def shares():
-        sv(1 - core).wait_recv()
+        came(pieces.at[pl.ds(0, 4)], u_recv.at[0])
         for r in range(8):
             for p in range(8):
                 table[r * 256 + p * PIECE:r * 256 + (p + 1) * PIECE, :] = pieces[p, r]
@@ -356,21 +350,19 @@
         share = (powers / jnp.sum(powers, axis=1, keepdims=True)).astype(jnp.bfloat16)
         for g, (first, width, axes) in enumerate(GROUPS):
             shares_out[g] = dot_nt(holder(g), share).astype(jnp.bfloat16)
-            weights[g, :, lane(g)] = shares_out[g, pl.ds(pl.multiple_of(at[axes[0]] * 32, 32), 32), :]
+            weights[g, :, own(g)] = shares_out[g, pl.ds(pl.multiple_of(at[axes[0]] * 32, 32), 32), :]
         for g in range(3):
             for i in (2, 1, 3):
                 sp(g, i).start()
 
     def prepare():
-        for g, (first, width, axes) in enumerate(GROUPS):
-            for i in (1, 2, 3):
-                sp(g, i, near(axes[0], -i)).wait_recv()
+        came(weights.at[:, :, pl.ds(0, 3 * TOK)], p_recv.at[0])
+        for g in range(3):
             total[g][...] = jnp.zeros(total[g].shape, jnp.float32)
 
-    for g, (first, width, axes) in enumerate(GROUPS):
-        for i in (1, 2, 3):
-            sq(g, i, near(axes[0], -i)).wait_recv()
-            s1(g, i, near(axes[0], -i)).wait_recv()
+    came(ranks.at[:, :, pl.ds(0, 3 * TOK)], q_recv.at[0])
+    for g in range(3):
+        came(blocks[g].at[pl.ds(0, 3 * TOK)], s1_recv.at[g])
 
     def step(k, carry):
         def stage(lag, run):
@@ -402,41 +394,18 @@
 
     lax.fori_loop(0, ROUNDS + 4, step, 0)
 
-    def leave(g):
-        first, width, axes = GROUPS[g]
-        return pltpu.make_async_copy(
-            normed.at[:, first:first + width], out.at[:, first:first + width], out_sem.at[g])
-
     for g, (first, width, axes) in enumerate(GROUPS):
-        result = total[g][own(g), :]
-        for i in (1, 2, 3):
-            r1(g, i).wait_recv()
-            result = result + back1[g][i - 1].astype(jnp.float32)
-        normed[:, first:first + width] = result.astype(jnp.bfloat16)
-        leave(g).start()
-
-    for i in (0, 1, 2, 3):
-        (su(i) if i else sv()).wait_send()
-    for i in range(1, 8):
-        st(i).wait_send()
+        came(parts.at[:, :, first:first + width], r1_recv.at[g])
+    went(pieces.at[pl.ds(0, 4)], u_send.at[0])
+    went(pieces.at[pl.ds(0, 3)], u_send.at[1])
+    went(pieces.at[0, pl.ds(0, 7)], t_send.at[0])
+    went(ranks.at[:, :, pl.ds(0, 3 * TOK)], q_send.at[0])
+    went(weights.at[:, :, pl.ds(0, 3 * TOK)], p_send.at[0])
     for g in range(3):
-        for i in (1, 2, 3):
-            sq(g, i).wait_send()
-            sp(g, i).wait_send()
-            r1(g, i).wait_send()
-
-    def drain(q, carry):
-        for g in range(3):
-            for i, d in PAIRS:
-                if i or d:
-                    s3(g, q, i, d).wait_send()
-                    r3(g, q, i, d).wait_send()
-            for i in (1, 2, 3):
-                r2(g, q, i).wait_send()
-        return carry
-
-    lax.fori_loop(0, ROUNDS, drain, 0)
-    for g in range(3):
+        went(hop2[g].at[:, :, pl.ds(0, 7)], s3_send.at[g])
+        went(hop2[g].at[:, :, pl.ds(0, 7)], r3_send.at[g])
+        went(back3[g].at[:, pl.ds(0, 3)], r2_send.at[g])
+        went(blocks[g].at[pl.ds(0, 3 * TOK)], r1_send.at[g])
         leave(g).wait()
 
 
@@ -445,7 +414,7 @@
 
 
 def flat_kernel(*refs):
-    args, rest = refs[:9], list(refs[9:])
+    args, rest = refs[:10], list(refs[10:])
 
     def take(n):
         head = rest[:n]
@@ -454,8 +423,8 @@
 
     blocks = take(3)
     ranks, weights = take(2)
-    packed, hop2, arrived, back3, back2, back1, total = (take(3) for _ in range(7))
-    kernel(*args, blocks, ranks, weights, packed, hop2, arrived, back3, back2, back1, total, *rest)
+    packed, hop2, arrived, back3, back2, total = (take(3) for _ in range(6))
+    kernel(*args, blocks, ranks, weights, packed, hop2, arrived, back3, back2, total, *rest)
 
 
 def per_device(tokens, norm_gain, router, routes, placement, w_gate, w_up, w_down):
@@ -469,7 +438,6 @@
         + per_group(lambda w: (ROUNDS, 8, 4, 16, w))
         + per_group(lambda w: (ROUNDS, 4, 8, 16, w))
         + per_group(lambda w: (ROUNDS, 4, 8, 16, w))
-        + per_group(lambda w: (3, TOK, w))
         + [pltpu.VMEM((SIDE * TOK, w), jnp.float32) for _, w, _ in GROUPS]
         + [
             pltpu.VMEM((WIDTH, HIDDEN), bf),
@@ -481,7 +449,7 @@
             pltpu.VMEM((SIDE * TOK, WIDTH), bf),
             pltpu.VMEM((SIDE * TOK, HIDDEN), bf),
             pltpu.VMEM((TOK, SIDE * TOK), jnp.float32),
-            pltpu.VMEM((SIDE * TOK, SIDE * TOK), bf),
+            pltpu.VMEM((3, SIDE * TOK, SIDE * TOK), bf),
             pltpu.VMEM((TOK, WIDTH), bf),
             pltpu.VMEM((1, WIDTH), jnp.float32),
             pltpu.VMEM((8, TOK), jnp.int32),
@@ -489,31 +457,36 @@
             pltpu.VMEM((3, DEVICES, TOK), bf),
             pltpu.VMEM((3, DEVICES, TOK), bf),
             dma((3,)), dma((5,)), dma((3,)),
-            dma((8,)), dma((8,)),
-            dma((4,)), dma((4,)),
-            dma((3, 4)), dma((3, 4)),
-            dma((3, 4)), dma((3, 4)),
-            dma((3, 4)), dma((3, 4)),
-            dma((3, ROUNDS, 4)), dma((3, ROUNDS, 4)),
-            dma((3, ROUNDS, 8)), dma((3, ROUNDS, 8)),
-            dma((3, ROUNDS, 8)), dma((3, ROUNDS, 8)),
-            dma((3, ROUNDS, 4)), dma((3, ROUNDS, 4)),
-            dma((3, 4)), dma((3, 4)),
+            dma((1,)), dma((1,)),
+            dma((2,)), dma((2,)),
+            dma((3,)), dma((3,)),
+            dma((1,)), dma((1,)),
+            dma((1,)), dma((1,)),
+            dma((3, ROUNDS)), dma((3, ROUNDS)),
+            dma((3,)), dma((3, ROUNDS)),
+            dma((3,)), dma((3, ROUNDS)),
+            dma((3,)), dma((3, ROUNDS)),
+            dma((3,)), dma((3,)),
         ]
     )
     whole = pl.BlockSpec(memory_space=pl.ANY)
-    return pl.pallas_call(
+    own_part, parts = pl.pallas_call(
         flat_kernel,
         name="moe",
-        out_shape=jax.ShapeDtypeStruct((TOK, WIDTH), bf),
+        out_shape=(
+            jax.ShapeDtypeStruct((TOK, WIDTH), jnp.float32),
+            jax.ShapeDtypeStruct((3, TOK, WIDTH), bf),
+        ),
         in_specs=[whole] * 8,
-        out_specs=whole,
+        out_specs=(whole, whole),
         scratch_shapes=scratch,
         compiler_params=pltpu.CompilerParams(
             collective_id=0, has_side_effects=True, vmem_limit_bytes=63 * 2**20
         ),
         cost_estimate=pl.CostEstimate(flops=15 * 10**9, bytes_accessed=11 * 10**6, transcendentals=10**6),
     )(tokens, norm_gain.reshape(1, WIDTH), router, routes.T, placement.reshape(1, DEVICES), w_gate, w_up, w_down)
+    one, two, three = (parts[i].astype(jnp.float32) for i in range(3))
+    return (own_part + one + two + three).astype(bf)
 
 
 def solution(mesh):

time: 136 us -> 131 us (0.963)
  Pallas kernels: 133 us -> 127 us
  other arithmetic: 0 us -> 2.75 us
  local copies, waits for them, and re-layouts: 1.88 us -> 0 us
    pallas_call x1, Pallas kernels: 133 us -> 127 us  [per_device(): pl.pallas_call(flat_kernel, name='moe', out_shape=(jax.ShapeDtypeStruct((...]
    convert_element_type x0 -> x1, other arithmetic: none -> 2.75 us  [per_device(): return (own_part + one + two + three).astype(bf)]
    unnamed x1 -> x0, local copies, waits for them, and re-layouts: 1.88 us -> none
where the time goes in v3:
time: 131 us; the launch traced here: 130 us
  Pallas kernels  127 us (97%)
  other arithmetic  2.75 us (2%)
    pallas_call x1, Pallas kernels, per_device(): pl.pallas_call(flat_kernel, name='moe', out_shape=(jax.ShapeDtypeStruct((...  127 us
    convert_element_type x1, other arithmetic, per_device(): return (own_part + one + two + three).astype(bf)  2.75 us

profile of v3, /device:TPU:0, one launch (start us, length us, event | category | flops | bytes accessed | tf_op | source)
XLA Modules:
  0.0 130.0 jit_solution(1410791415653520988)
XLA Ops:
  0.0 127.2 %moe.1 = (f32[128,2048]{1,0:T(8,128)}, bf16[3,128,2048]{2,1,0:T(8,128)(2,1)}) custom-call(bf16[128,2048]{1,0:T(8,128)(2,1)} %refs_0_.1, f32[1,2048]{1,0:T(1,128)} %bitcast.12, bf16[256,128]{1,0:T(8,128)(2,1)} %refs_2_.1, s32[8,128]{1,0:T(8,128)} %bitcast.13, s32[1,128]{1,0:T(1,128)} %bitcast.14, bf16[1,2048,768]{2,1,0:T(8,128)(2,1)} %refs_5_.1, ...), custom_call_target="tpu_custom_call" | custom-call | flops 15000000512 | bytes 11000000 | tf_op jit(solution)/shard_map/moe/pallas_call | solution.py:473
  127.2 2.8 %fusion = bf16[128,2048]{1,0:T(8,128)(2,1)} fusion(f32[128,2048]{1,0:T(8,128)} %get-tuple-element.7, bf16[3,128,2048]{2,1,0:T(8,128)(2,1)} %get-tuple-element.8), kind=kLoop, calls=%fused_computation.1 | loop fusion | flops 1835008 | bytes 3145728 | tf_op jit(solution)/shard_map/convert_element_type | solution.py:489

commit v4 on v3

--- a/solution.py
+++ b/solution.py
@@ -21,6 +21,7 @@
 NT = (((1,), (1,)), ((), ()))
 TN = (((0,), (0,)), ((), ()))
 PIECE = 32
+HALF = 384
 
 
 def iota(shape, dim):
@@ -40,7 +41,7 @@
 
 
 def kernel(
-    tokens, gain, router, routes, placement, w_gate, w_up, w_down, own_out, parts,
+    tokens, gain, router, routes, placement, w_gate, w_up, w_down, parts,
     blocks, ranks, weights, packed, hop2, arrived, back3, back2, total,
     gate_v, up_v, down_v, normed, table, pieces, stacked, hidden, slot_of, mix,
     tokens_v, gain_v, routes_v, placement_v, ranks_out, shares_out,
@@ -146,9 +147,13 @@
     def own(g):
         return block(g, at[GROUPS[g][2][0]])
 
-    def s1(g, i):
+    def half(g, h):
+        return slice(0, HALF) if h == 0 else slice(HALF, GROUPS[g][1])
+
+    def s1(g, i, h):
         a = GROUPS[g][2][0]
-        return remote(blocks[g].at[own(g)], blocks[g].at[own(g)], s1_send.at[g], s1_recv.at[g],
+        mine = blocks[g].at[own(g), half(g, h)]
+        return remote(mine, mine, s1_send.at[g], s1_recv.at[g, h],
                       along(a, near(a, i), core))
 
     def sq(g, i):
@@ -177,10 +182,13 @@
 
     for i in (2, 1, 3):
         for g in range(3):
-            s1(g, i).start()
+            s1(g, i, 0).start()
     for g in range(3):
         for i in (2, 1, 3):
             sq(g, i).start()
+    for i in (2, 1, 3):
+        for g in range(3):
+            s1(g, i, 1).start()
     for i in range(1, 8):
         st(i).start()
 
@@ -203,10 +211,10 @@
             wanted = a * 64 + d * 16 + b * 4 + s
         return jnp.where(c == wanted, 1.0, 0.0).astype(jnp.bfloat16)
 
-    def s2(g, q, i):
+    def s2(g, q, i, cols):
         a = GROUPS[g][2][1]
         v = near(a, i)
-        return remote(packed[g].at[q, pl.ds(v * 8, 8)], hop2[g].at[q, at[a]],
+        return remote(packed[g].at[q, pl.ds(v * 8, 8), :, cols], hop2[g].at[q, at[a], :, :, cols],
                       s2_send.at[g, q], s2_recv.at[g, q], along(a, v, core))
 
     def s3(g, q, i, d):
@@ -227,35 +235,50 @@
             return pltpu.make_async_copy(src, dst, r3_recv.at[g, q])
         return remote(src, dst, r3_send.at[g], r3_recv.at[g, q], along(a, u, c))
 
-    def r2(g, q, i):
+    def r2(g, q, i, h):
         a = GROUPS[g][2][1]
         v = near(a, i)
-        src, dst = back3[g].at[q, v], back2[g].at[q, at[a]]
+        cols = half(g, h)
+        src, dst = back3[g].at[q, v, :, :, cols], back2[g].at[q, at[a], :, :, cols]
         if i == 0:
-            return pltpu.make_async_copy(src, dst, r2_recv.at[g, q])
-        return remote(src, dst, r2_send.at[g], r2_recv.at[g, q], along(a, v, core))
-
-    def r1(g, i):
+            return pltpu.make_async_copy(src, dst, r2_recv.at[g, q, h])
+        return remote(src, dst, r2_send.at[g], r2_recv.at[g, q, h], along(a, v, core))
+
+    def r1(g, i, h):
         first, width, axes = GROUPS[g]
         a = axes[0]
-        return remote(blocks[g].at[block(g, near(a, i))], parts.at[i - 1, :, first:first + width], r1_send.at[g], r1_recv.at[g],
+        cols = half(g, h)
+        return remote(blocks[g].at[block(g, near(a, i)), cols],
+                      parts.at[i - 1, :, first + cols.start:first + cols.stop], r1_send.at[g], r1_recv.at[g],
                       along(a, near(a, i), core))
 
     PAIRS = [(i, d) for i in (2, 1, 3, 0) for d in (0, 1)]
 
-    def gather(q):
-        slot = slot_of[...] + (q * SLOTS).astype(jnp.float32)
+    def choose(q):
+        slot = slot_of[...] + jnp.asarray(q * SLOTS, jnp.float32)
+        for i in range(SIDE):
+            for g, (first, width, axes) in enumerate(GROUPS):
+                mix[g, i * TOK:(i + 1) * TOK, :] = jnp.where(
+                    spread(near(axes[1], i), ranks[g]) == slot, 1.0, 0.0).astype(jnp.bfloat16)
+
+    def gather(q, h):
         for i in (2, 1, 3, 0):
             for g, (first, width, axes) in enumerate(GROUPS):
                 v = near(axes[1], i)
-                found = spread(v, ranks[g])
-                pick = jnp.where(found == slot, 1.0, 0.0).astype(jnp.bfloat16)
-                rows = dot(pick, blocks[g][...]).astype(jnp.bfloat16).reshape(8, 16, width)
+                cols = slice(0, width) if h is None else half(g, h)
+                rows = dot(mix[g, i * TOK:(i + 1) * TOK, :], blocks[g][:, cols])
+                rows = rows.astype(jnp.bfloat16).reshape(8, 16, cols.stop - cols.start)
                 if i == 0:
-                    hop2[g][q, v] = rows
+                    hop2[g][q, v, :, :, cols] = rows
                 else:
-                    packed[g][q, pl.ds(v * 8, 8)] = rows
-                    s2(g, q, i).start()
+                    packed[g][q, pl.ds(v * 8, 8), :, cols] = rows
+                    s2(g, q, i, cols).start()
+
+    def whole_gather(q):
+        @pl.when(q > 0)
+        def _():
+            choose(q)
+            gather(q, None)
 
     def forward(q):
         for g in range(3):
@@ -301,15 +324,17 @@
                 r3(g, q, i, d).start()
 
     def back(q):
-        for g, (first, width, axes) in enumerate(GROUPS):
+        for g in range(3):
             came(back3[g].at[q], r3_recv.at[g, q])
+        for h in (0, 1):
             for i in (2, 1, 3, 0):
-                r2(g, q, i).start()
+                for g in range(3):
+                    r2(g, q, i, h).start()
 
     def leave(g):
         first, width, axes = GROUPS[g]
         return pltpu.make_async_copy(
-            total[g].at[own(g)], own_out.at[:, first:first + width], out_sem.at[g])
+            blocks[g].at[own(g)], parts.at[3, :, first:first + width], out_sem.at[g])
 
     def combine(q):
         slot = slot_of[...] + (q * SLOTS).astype(jnp.float32)
@@ -317,17 +342,22 @@
             for v in range(SIDE):
                 mix[g, v * TOK:(v + 1) * TOK, :] = jnp.where(
                     spread(v, ranks[g]) == slot, spread(v, weights[g]), 0.0).astype(jnp.bfloat16)
-        for g, (first, width, axes) in enumerate(GROUPS):
-            came(back2[g].at[q], r2_recv.at[g, q])
-            total[g][...] += dot_tn(mix[g], back2[g][q].reshape(SIDE * TOK, width))
-
-            @pl.when(q == ROUNDS - 1)
-            def _():
-                went(blocks[g].at[pl.ds(0, 3 * TOK)], s1_send.at[g])
-                blocks[g][...] = total[g][...].astype(jnp.bfloat16)
-                for i in (2, 1, 3):
-                    r1(g, i).start()
-                leave(g).start()
+        for h in (0, 1):
+            for g, (first, width, axes) in enumerate(GROUPS):
+                cols = half(g, h)
+                came(back2[g].at[q, :, :, :, cols], r2_recv.at[g, q, h])
+                total[g][:, cols] += dot_tn(
+                    mix[g], back2[g][q, :, :, :, cols].reshape(SIDE * TOK, cols.stop - cols.start))
+
+                @pl.when(q == ROUNDS - 1)
+                def _():
+                    if h == 0:
+                        went(blocks[g].at[pl.ds(0, 3 * TOK)], s1_send.at[g])
+                    blocks[g][:, cols] = total[g][:, cols].astype(jnp.bfloat16)
+                    for i in (2, 1, 3):
+                        r1(g, i, h).start()
+                    if h == 1:
+                        leave(g).start()
 
     def along_x():
         came(pieces.at[mine, pl.ds(0, 7)], t_recv.at[0])
@@ -361,8 +391,11 @@
             total[g][...] = jnp.zeros(total[g].shape, jnp.float32)
 
     came(ranks.at[:, :, pl.ds(0, 3 * TOK)], q_recv.at[0])
-    for g in range(3):
-        came(blocks[g].at[pl.ds(0, 3 * TOK)], s1_recv.at[g])
+    choose(0)
+    for h in (0, 1):
+        for g in range(3):
+            came(blocks[g].at[pl.ds(0, 3 * TOK), half(g, h)], s1_recv.at[g, h])
+        gather(0, h)
 
     def step(k, carry):
         def stage(lag, run):
@@ -375,7 +408,7 @@
             def _():
                 run()
 
-        stage(0, gather)
+        stage(0, whole_gather)
         once(0, along_x)
         once(1, across)
         stage(1, forward)
@@ -395,7 +428,7 @@
     lax.fori_loop(0, ROUNDS + 4, step, 0)
 
     for g, (first, width, axes) in enumerate(GROUPS):
-        came(parts.at[:, :, first:first + width], r1_recv.at[g])
+        came(parts.at[pl.ds(0, 3), :, first:first + width], r1_recv.at[g])
     went(pieces.at[pl.ds(0, 4)], u_send.at[0])
     went(pieces.at[pl.ds(0, 3)], u_send.at[1])
     went(pieces.at[0, pl.ds(0, 7)], t_send.at[0])
@@ -414,7 +447,7 @@
 
 
 def flat_kernel(*refs):
-    args, rest = refs[:10], list(refs[10:])
+    args, rest = refs[:9], list(refs[9:])
 
     def take(n):
         head = rest[:n]
@@ -459,34 +492,31 @@
             dma((3,)), dma((5,)), dma((3,)),
             dma((1,)), dma((1,)),
             dma((2,)), dma((2,)),
-            dma((3,)), dma((3,)),
+            dma((3,)), dma((3, 2)),
             dma((1,)), dma((1,)),
             dma((1,)), dma((1,)),
             dma((3, ROUNDS)), dma((3, ROUNDS)),
             dma((3,)), dma((3, ROUNDS)),
             dma((3,)), dma((3, ROUNDS)),
-            dma((3,)), dma((3, ROUNDS)),
+            dma((3,)), dma((3, ROUNDS, 2)),
             dma((3,)), dma((3,)),
         ]
     )
     whole = pl.BlockSpec(memory_space=pl.ANY)
-    own_part, parts = pl.pallas_call(
+    parts = pl.pallas_call(
         flat_kernel,
         name="moe",
-        out_shape=(
-            jax.ShapeDtypeStruct((TOK, WIDTH), jnp.float32),
-            jax.ShapeDtypeStruct((3, TOK, WIDTH), bf),
-        ),
+        out_shape=jax.ShapeDtypeStruct((SIDE, TOK, WIDTH), bf),
         in_specs=[whole] * 8,
-        out_specs=(whole, whole),
+        out_specs=whole,
         scratch_shapes=scratch,
         compiler_params=pltpu.CompilerParams(
             collective_id=0, has_side_effects=True, vmem_limit_bytes=63 * 2**20
         ),
         cost_estimate=pl.CostEstimate(flops=15 * 10**9, bytes_accessed=11 * 10**6, transcendentals=10**6),
     )(tokens, norm_gain.reshape(1, WIDTH), router, routes.T, placement.reshape(1, DEVICES), w_gate, w_up, w_down)
-    one, two, three = (parts[i].astype(jnp.float32) for i in range(3))
-    return (own_part + one + two + three).astype(bf)
+    one, two, three, own = (parts[i].astype(jnp.float32) for i in range(SIDE))
+    return (own + one + two + three).astype(bf)
 
 
 def solution(mesh):

time: 131 us -> 125 us (0.954)
  Pallas kernels: 127 us -> 121 us
    pallas_call x1, Pallas kernels: 127 us -> 121 us  [per_device(): pl.pallas_call(flat_kernel, name='moe', out_shape=jax.ShapeDtypeStruct((S...]
    convert_element_type x1 -> x0, other arithmetic: 2.75 us -> none  [per_device(): return (own_part + one + two + three).astype(bf)]
    add x0 -> x1, other arithmetic: none -> 2.65 us  [per_device(): return (own + one + two + three).astype(bf)]
where the time goes in v4:
time: 125 us; the launch traced here: 124 us
  Pallas kernels  121 us (97%)
  other arithmetic  2.65 us (2%)
    pallas_call x1, Pallas kernels, per_device(): pl.pallas_call(flat_kernel, name='moe', out_shape=jax.ShapeDtypeStruct((S...  121 us
    add x1, other arithmetic, per_device(): return (own + one + two + three).astype(bf)  2.65 us

profile of v4, /device:TPU:0, one launch (start us, length us, event | category | flops | bytes accessed | tf_op | source)
XLA Modules:
  0.0 123.5 jit_solution(921682978703941281)
XLA Ops:
  0.0 120.8 %moe.1 = bf16[4,128,2048]{2,1,0:T(8,128)(2,1)} custom-call(bf16[128,2048]{1,0:T(8,128)(2,1)} %refs_0_.1, f32[1,2048]{1,0:T(1,128)} %bitcast.5, bf16[256,128]{1,0:T(8,128)(2,1)} %refs_2_.1, s32[8,128]{1,0:T(8,128)} %bitcast.6, s32[1,128]{1,0:T(1,128)} %bitcast.7, bf16[1,2048,768]{2,1,0:T(8,128)(2,1)} %refs_5_.1, bf16[1,2048,768]{2,1,0:T(8,128)(2,1)} %refs_6_.1, ...), custom_call_target="tpu_custom_call" | custom-call | flops 15000000512 | bytes 11000000 | tf_op jit(solution)/shard_map/moe/pallas_call | solution.py:506
  120.9 2.6 %fusion = bf16[128,2048]{1,0:T(8,128)(2,1)} fusion(bf16[4,128,2048]{2,1,0:T(8,128)(2,1)} %moe.1), kind=kLoop, calls=%fused_computation.1 | loop fusion | flops 2097152 | bytes 2621440 | tf_op jit(solution)/shard_map/add | solution.py:519

commit v5 on v4

--- a/solution.py
+++ b/solution.py
@@ -19,7 +19,6 @@
     (1408, 640, (1, 2, 0)),
 )
 NT = (((1,), (1,)), ((), ()))
-TN = (((0,), (0,)), ((), ()))
 PIECE = 32
 HALF = 384
 
@@ -36,17 +35,13 @@
     return lax.dot_general(a, b, NT, preferred_element_type=jnp.float32)
 
 
-def dot_tn(a, b):
-    return lax.dot_general(a, b, TN, preferred_element_type=jnp.float32)
-
-
 def kernel(
-    tokens, gain, router, routes, placement, w_gate, w_up, w_down, parts,
-    blocks, ranks, weights, packed, hop2, arrived, back3, back2, total,
+    tokens, gain, router, routes, placement, w_gate, w_up, w_down, own_part, low_part, high_part,
+    blocks, ranks, weights, packed, hop2, arrived, back3, back2, passing, total,
     gate_v, up_v, down_v, normed, table, pieces, stacked, hidden, slot_of, mix,
     tokens_v, gain_v, routes_v, placement_v, ranks_out, shares_out,
     w_sem, in_sem, out_sem, t_send, t_recv, u_send, u_recv,
-    s1_send, s1_recv, q_send, q_recv, p_send, p_recv, s2_send, s2_recv, s3_send, s3_recv, r3_send, r3_recv, r2_send, r2_recv, r1_send, r1_recv,
+    s1_send, s1_recv, q_send, q_recv, p_send, p_recv, s2_send, s2_recv, s3_send, s3_recv, r3_send, r3_recv, r2_send, r2_recv, r1_send, r1_recv, f_recv,
 ):
     rep = lax.axis_index("rep")
     exp = lax.axis_index("expert")
@@ -244,13 +239,20 @@
             return pltpu.make_async_copy(src, dst, r2_recv.at[g, q, h])
         return remote(src, dst, r2_send.at[g], r2_recv.at[g, q, h], along(a, v, core))
 
-    def r1(g, i, h):
+    def far(g, h):
+        a = GROUPS[g][2][0]
+        cols = half(g, h)
+        return remote(blocks[g].at[block(g, near(a, 2)), cols], passing[g].at[:, cols],
+                      r1_send.at[g], f_recv.at[g, h], along(a, near(a, 1 if h == 0 else 3), core))
+
+    def home(g, h, up):
         first, width, axes = GROUPS[g]
         a = axes[0]
         cols = half(g, h)
-        return remote(blocks[g].at[block(g, near(a, i)), cols],
-                      parts.at[i - 1, :, first + cols.start:first + cols.stop], r1_send.at[g], r1_recv.at[g],
-                      along(a, near(a, i), core))
+        v = near(a, 1 if up else 3)
+        part = low_part if up else high_part
+        return remote(blocks[g].at[block(g, v), cols], part.at[:, first + cols.start:first + cols.stop],
+                      r1_send.at[g], r1_recv.at[g], along(a, v, core))
 
     PAIRS = [(i, d) for i in (2, 1, 3, 0) for d in (0, 1)]
 
@@ -334,19 +336,19 @@
     def leave(g):
         first, width, axes = GROUPS[g]
         return pltpu.make_async_copy(
-            blocks[g].at[own(g)], parts.at[3, :, first:first + width], out_sem.at[g])
+            blocks[g].at[own(g)], own_part.at[:, first:first + width], out_sem.at[g])
 
     def combine(q):
         slot = slot_of[...] + (q * SLOTS).astype(jnp.float32)
         for g in range(3):
             for v in range(SIDE):
-                mix[g, v * TOK:(v + 1) * TOK, :] = jnp.where(
-                    spread(v, ranks[g]) == slot, spread(v, weights[g]), 0.0).astype(jnp.bfloat16)
+                mix[g, :, v * TOK:(v + 1) * TOK] = jnp.transpose(jnp.where(
+                    spread(v, ranks[g]) == slot, spread(v, weights[g]), 0.0)).astype(jnp.bfloat16)
         for h in (0, 1):
             for g, (first, width, axes) in enumerate(GROUPS):
                 cols = half(g, h)
                 came(back2[g].at[q, :, :, :, cols], r2_recv.at[g, q, h])
-                total[g][:, cols] += dot_tn(
+                total[g][:, cols] += dot(
                     mix[g], back2[g][q, :, :, :, cols].reshape(SIDE * TOK, cols.stop - cols.start))
 
                 @pl.when(q == ROUNDS - 1)
@@ -354,8 +356,8 @@
                     if h == 0:
                         went(blocks[g].at[pl.ds(0, 3 * TOK)], s1_send.at[g])
                     blocks[g][:, cols] = total[g][:, cols].astype(jnp.bfloat16)
-                    for i in (2, 1, 3):
-                        r1(g, i, h).start()
+                    far(g, h).start()
+                    home(g, h, h == 1).start()
                     if h == 1:
                         leave(g).start()
 
@@ -427,8 +429,16 @@
 
     lax.fori_loop(0, ROUNDS + 4, step, 0)
 
-    for g, (first, width, axes) in enumerate(GROUPS):
-        came(parts.at[pl.ds(0, 3), :, first:first + width], r1_recv.at[g])
+    for h in (0, 1):
+        for g, (first, width, axes) in enumerate(GROUPS):
+            cols = half(g, h)
+            came(passing[g].at[:, cols], f_recv.at[g, h])
+            rows = block(g, near(axes[0], 1 if h == 0 else 3))
+            both = total[g][rows, cols] + passing[g][:, cols].astype(jnp.float32)
+            blocks[g][rows, cols] = both.astype(jnp.bfloat16)
+            home(g, h, h == 0).start()
+    for g in range(3):
+        came(blocks[g].at[pl.ds(0, 2 * TOK)], r1_recv.at[g])
     went(pieces.at[pl.ds(0, 4)], u_send.at[0])
     went(pieces.at[pl.ds(0, 3)], u_send.at[1])
     went(pieces.at[0, pl.ds(0, 7)], t_send.at[0])
@@ -447,7 +457,7 @@
 
 
 def flat_kernel(*refs):
-    args, rest = refs[:9], list(refs[9:])
+    args, rest = refs[:11], list(refs[11:])
 
     def take(n):
         head = rest[:n]
@@ -456,8 +466,8 @@
 
     blocks = take(3)
     ranks, weights = take(2)
-    packed, hop2, arrived, back3, back2, total = (take(3) for _ in range(6))
-    kernel(*args, blocks, ranks, weights, packed, hop2, arrived, back3, back2, total, *rest)
+    packed, hop2, arrived, back3, back2, passing, total = (take(3) for _ in range(7))
+    kernel(*args, blocks, ranks, weights, packed, hop2, arrived, back3, back2, passing, total, *rest)
 
 
 def per_device(tokens, norm_gain, router, routes, placement, w_gate, w_up, w_down):
@@ -471,6 +481,7 @@
         + per_group(lambda w: (ROUNDS, 8, 4, 16, w))
         + per_group(lambda w: (ROUNDS, 4, 8, 16, w))
         + per_group(lambda w: (ROUNDS, 4, 8, 16, w))
+        + per_group(lambda w: (TOK, w))
         + [pltpu.VMEM((SIDE * TOK, w), jnp.float32) for _, w, _ in GROUPS]
         + [
             pltpu.VMEM((WIDTH, HIDDEN), bf),
@@ -499,24 +510,23 @@
             dma((3,)), dma((3, ROUNDS)),
             dma((3,)), dma((3, ROUNDS)),
             dma((3,)), dma((3, ROUNDS, 2)),
-            dma((3,)), dma((3,)),
+            dma((3,)), dma((3,)), dma((3, 2)),
         ]
     )
     whole = pl.BlockSpec(memory_space=pl.ANY)
-    parts = pl.pallas_call(
+    own, low, high = pl.pallas_call(
         flat_kernel,
         name="moe",
-        out_shape=jax.ShapeDtypeStruct((SIDE, TOK, WIDTH), bf),
+        out_shape=[jax.ShapeDtypeStruct((TOK, WIDTH), bf)] * 3,
         in_specs=[whole] * 8,
-        out_specs=whole,
+        out_specs=[whole] * 3,
         scratch_shapes=scratch,
         compiler_params=pltpu.CompilerParams(
             collective_id=0, has_side_effects=True, vmem_limit_bytes=63 * 2**20
         ),
         cost_estimate=pl.CostEstimate(flops=15 * 10**9, bytes_accessed=11 * 10**6, transcendentals=10**6),
     )(tokens, norm_gain.reshape(1, WIDTH), router, routes.T, placement.reshape(1, DEVICES), w_gate, w_up, w_down)
-    one, two, three, own = (parts[i].astype(jnp.float32) for i in range(SIDE))
-    return (own + one + two + three).astype(bf)
+    return (own.astype(jnp.float32) + low.astype(jnp.float32) + high.astype(jnp.float32)).astype(bf)
 
 
 def solution(mesh):

time: 125 us -> 123 us (0.984); the launches traced: 124 us -> 123 us
    add x1 -> x0, other arithmetic: 2.65 us -> none  [per_device(): return (own + one + two + three).astype(bf)]
    convert_element_type x0 -> x1, other arithmetic: none -> 2.4 us  [per_device(): (own.astype(jnp.float32) + low.astype(jnp.float32) + high.astype(jnp.floa...]
where the time goes in v5:
time: 123 us
  Pallas kernels  121 us (98%)
  other arithmetic  2.4 us (2%)
    pallas_call x1, Pallas kernels, per_device(): pl.pallas_call(flat_kernel, name='moe', out_shape=[jax.ShapeDtypeStruct((...  121 us

profile of v5, /device:TPU:0, one launch (start us, length us, event | category | flops | bytes accessed | tf_op | source)
XLA Modules:
  0.0 123.0 jit_solution(14046568511676431262)
XLA Ops:
  0.0 120.6 %moe.1 = (bf16[128,2048]{1,0:T(8,128)(2,1)}, bf16[128,2048]{1,0:T(8,128)(2,1)}, bf16[128,2048]{1,0:T(8,128)(2,1)}) custom-call(bf16[128,2048]{1,0:T(8,128)(2,1)} %refs_0_.1, f32[1,2048]{1,0:T(1,128)} %bitcast.3, bf16[256,128]{1,0:T(8,128)(2,1)} %refs_2_.1, s32[8,128]{1,0:T(8,128)} %bitcast.4, s32[1,128]{1,0:T(1,128)} %bitcast.5, ...), custom_call_target="tpu_custom_call" | custom-call | flops 15000000512 | bytes 11000000 | tf_op jit(solution)/shard_map/moe/pallas_call | solution.py:517
  120.7 2.4 %add_convert_fusion = bf16[128,2048]{1,0:T(8,128)(2,1)} fusion(bf16[128,2048]{1,0:T(8,128)(2,1)} %get-tuple-element.10, bf16[128,2048]{1,0:T(8,128)(2,1)} %get-tuple-element.9, bf16[128,2048]{1,0:T(8,128)(2,1)} %get-tuple-element.8), kind=kLoop, calls=%fused_computation | loop fusion | flops 1572864 | bytes 2097152 | tf_op jit(solution)/shard_map/convert_element_type | solution.py:529

commit v6 on v5

--- a/solution.py
+++ b/solution.py
@@ -148,7 +148,7 @@
     def s1(g, i, h):
         a = GROUPS[g][2][0]
         mine = blocks[g].at[own(g), half(g, h)]
-        return remote(mine, mine, s1_send.at[g], s1_recv.at[g, h],
+        return remote(mine, mine, s1_send.at[g], s1_recv.at[h],
                       along(a, near(a, i), core))
 
     def sq(g, i):
@@ -210,7 +210,7 @@
         a = GROUPS[g][2][1]
         v = near(a, i)
         return remote(packed[g].at[q, pl.ds(v * 8, 8), :, cols], hop2[g].at[q, at[a], :, :, cols],
-                      s2_send.at[g, q], s2_recv.at[g, q], along(a, v, core))
+                      s2_send.at[q], s2_recv.at[g, q], along(a, v, core))
 
     def s3(g, q, i, d):
         a = GROUPS[g][2][2]
@@ -218,8 +218,8 @@
         src = hop2[g].at[q, :, u * 2 + c]
         dst = arrived[g].at[q, core * 4 + at[a]]
         if i == 0 and d == 0:
-            return pltpu.make_async_copy(src, dst, s3_recv.at[g, q])
-        return remote(src, dst, s3_send.at[g], s3_recv.at[g, q], along(a, u, c))
+            return pltpu.make_async_copy(src, dst, s3_recv.at[q])
+        return remote(src, dst, s3_send.at[g], s3_recv.at[q], along(a, u, c))
 
     def r3(g, q, i, d):
         a = GROUPS[g][2][2]
@@ -227,8 +227,8 @@
         src = packed[g].at[q, pl.ds((c * 4 + u) * 4, 4)]
         dst = back3[g].at[q, :, at[a] * 2 + core]
         if i == 0 and d == 0:
-            return pltpu.make_async_copy(src, dst, r3_recv.at[g, q])
-        return remote(src, dst, r3_send.at[g], r3_recv.at[g, q], along(a, u, c))
+            return pltpu.make_async_copy(src, dst, r3_recv.at[q])
+        return remote(src, dst, r3_send.at[g], r3_recv.at[q], along(a, u, c))
 
     def r2(g, q, i, h):
         a = GROUPS[g][2][1]
@@ -290,7 +290,8 @@
 
     def expert(q):
         for g, (first, width, axes) in enumerate(GROUPS):
-            came(arrived[g].at[q], s3_recv.at[g, q])
+            if g == 0:
+                came(stacked, s3_recv.at[q])
             for c in (0, 1):
                 part = arrived[g][q, pl.ds(c * 4, 4)]
                 if axes[0] == 2:
@@ -312,7 +313,8 @@
         lax.fori_loop(0, HIDDEN // 256, tile, 0)
         for g, (first, width, axes) in enumerate(GROUPS):
             result = dot(hidden[...], down_v[:, first:first + width]).astype(jnp.bfloat16)
-            went(packed[g].at[q, pl.ds(0, 24)], s2_send.at[g, q])
+            if g == 0:
+                went(stacked.at[pl.ds(0, 3 * TOK)], s2_send.at[q])
             for c in (0, 1):
                 half = result[c * 256:(c + 1) * 256]
                 if axes[0] == 2:
@@ -326,8 +328,7 @@
                 r3(g, q, i, d).start()
 
     def back(q):
-        for g in range(3):
-            came(back3[g].at[q], r3_recv.at[g, q])
+        came(stacked, r3_recv.at[q])
         for h in (0, 1):
             for i in (2, 1, 3, 0):
                 for g in range(3):
@@ -395,8 +396,7 @@
     came(ranks.at[:, :, pl.ds(0, 3 * TOK)], q_recv.at[0])
     choose(0)
     for h in (0, 1):
-        for g in range(3):
-            came(blocks[g].at[pl.ds(0, 3 * TOK), half(g, h)], s1_recv.at[g, h])
+        came(stacked.at[pl.ds(0, 3 * TOK), slice(0, 3 * HALF) if h == 0 else slice(3 * HALF, WIDTH)], s1_recv.at[h])
         gather(0, h)
 
     def step(k, carry):
@@ -422,12 +422,12 @@
                 load.wait()
 
         stage(2, expert)
+        once(3, prepare)
         stage(3, back)
-        once(3, prepare)
-        stage(4, combine)
+        stage(5, combine)
         return carry
 
-    lax.fori_loop(0, ROUNDS + 4, step, 0)
+    lax.fori_loop(0, ROUNDS + 5, step, 0)
 
     for h in (0, 1):
         for g, (first, width, axes) in enumerate(GROUPS):
@@ -503,12 +503,12 @@
             dma((3,)), dma((5,)), dma((3,)),
             dma((1,)), dma((1,)),
             dma((2,)), dma((2,)),
-            dma((3,)), dma((3, 2)),
+            dma((3,)), dma((2,)),
             dma((1,)), dma((1,)),
             dma((1,)), dma((1,)),
-            dma((3, ROUNDS)), dma((3, ROUNDS)),
-            dma((3,)), dma((3, ROUNDS)),
-            dma((3,)), dma((3, ROUNDS)),
+            dma((ROUNDS,)), dma((3, ROUNDS)),
+            dma((3,)), dma((ROUNDS,)),
+            dma((3,)), dma((ROUNDS,)),
             dma((3,)), dma((3, ROUNDS, 2)),
             dma((3,)), dma((3,)), dma((3, 2)),
         ]

time: 123 us -> 123 us (level)
  no operation moved by 1% of the time
where the time goes in v6:
time: 123 us; the launch traced here: 122 us
  Pallas kernels  120 us (98%)
  other arithmetic  2.4 us (2%)
    pallas_call x1, Pallas kernels, per_device(): pl.pallas_call(flat_kernel, name='moe', out_shape=[jax.ShapeDtypeStruct((...  120 us

profile of v6, /device:TPU:0, one launch (start us, length us, event | category | flops | bytes accessed | tf_op | source)
XLA Modules:
  0.0 122.5 jit_solution(17711805532010282921)
XLA Ops:
  0.0 120.1 %moe.1 = (bf16[128,2048]{1,0:T(8,128)(2,1)}, bf16[128,2048]{1,0:T(8,128)(2,1)}, bf16[128,2048]{1,0:T(8,128)(2,1)}) custom-call(bf16[128,2048]{1,0:T(8,128)(2,1)} %refs_0_.1, f32[1,2048]{1,0:T(1,128)} %bitcast.3, bf16[256,128]{1,0:T(8,128)(2,1)} %refs_2_.1, s32[8,128]{1,0:T(8,128)} %bitcast.4, s32[1,128]{1,0:T(1,128)} %bitcast.5, ...), custom_call_target="tpu_custom_call" | custom-call | flops 15000000512 | bytes 11000000 | tf_op jit(solution)/shard_map/moe/pallas_call | solution.py:517
  120.1 2.4 %add_convert_fusion = bf16[128,2048]{1,0:T(8,128)(2,1)} fusion(bf16[128,2048]{1,0:T(8,128)(2,1)} %get-tuple-element.10, bf16[128,2048]{1,0:T(8,128)(2,1)} %get-tuple-element.9, bf16[128,2048]{1,0:T(8,128)(2,1)} %get-tuple-element.8), kind=kLoop, calls=%fused_computation | loop fusion | flops 1572864 | bytes 2097152 | tf_op jit(solution)/shard_map/convert_element_type | solution.py:529

commit v7 on v6

--- a/solution.py
+++ b/solution.py
@@ -264,16 +264,16 @@
                     spread(near(axes[1], i), ranks[g]) == slot, 1.0, 0.0).astype(jnp.bfloat16)
 
     def gather(q, h):
-        for i in (2, 1, 3, 0):
-            for g, (first, width, axes) in enumerate(GROUPS):
+        for g, (first, width, axes) in enumerate(GROUPS):
+            cols = slice(0, width) if h is None else half(g, h)
+            rows = dot(mix[g], blocks[g][:, cols]).astype(jnp.bfloat16)
+            rows = rows.reshape(SIDE, 8, 16, cols.stop - cols.start)
+            for i in (2, 1, 3, 0):
                 v = near(axes[1], i)
-                cols = slice(0, width) if h is None else half(g, h)
-                rows = dot(mix[g, i * TOK:(i + 1) * TOK, :], blocks[g][:, cols])
-                rows = rows.astype(jnp.bfloat16).reshape(8, 16, cols.stop - cols.start)
                 if i == 0:
-                    hop2[g][q, v, :, :, cols] = rows
+                    hop2[g][q, v, :, :, cols] = rows[i]
                 else:
-                    packed[g][q, pl.ds(v * 8, 8), :, cols] = rows
+                    packed[g][q, pl.ds(v * 8, 8), :, cols] = rows[i]
                     s2(g, q, i, cols).start()
 
     def whole_gather(q):

time: 123 us -> 123 us (level)
  no operation moved by 1% of the time
where the time goes in v7:
time: 123 us
  Pallas kernels  121 us (98%)
  other arithmetic  2.4 us (2%)
    pallas_call x1, Pallas kernels, per_device(): pl.pallas_call(flat_kernel, name='moe', out_shape=[jax.ShapeDtypeStruct((...  121 us

profile of v7, /device:TPU:0, one launch (start us, length us, event | category | flops | bytes accessed | tf_op | source)
XLA Modules:
  0.0 123.1 jit_solution(18429090966455745831)
XLA Ops:
  0.0 120.7 %moe.1 = (bf16[128,2048]{1,0:T(8,128)(2,1)}, bf16[128,2048]{1,0:T(8,128)(2,1)}, bf16[128,2048]{1,0:T(8,128)(2,1)}) custom-call(bf16[128,2048]{1,0:T(8,128)(2,1)} %refs_0_.1, f32[1,2048]{1,0:T(1,128)} %bitcast.3, bf16[256,128]{1,0:T(8,128)(2,1)} %refs_2_.1, s32[8,128]{1,0:T(8,128)} %bitcast.4, s32[1,128]{1,0:T(1,128)} %bitcast.5, ...), custom_call_target="tpu_custom_call" | custom-call | flops 15000000512 | bytes 11000000 | tf_op jit(solution)/shard_map/moe/pallas_call | solution.py:517
  120.7 2.4 %add_convert_fusion = bf16[128,2048]{1,0:T(8,128)(2,1)} fusion(bf16[128,2048]{1,0:T(8,128)(2,1)} %get-tuple-element.10, bf16[128,2048]{1,0:T(8,128)(2,1)} %get-tuple-element.9, bf16[128,2048]{1,0:T(8,128)(2,1)} %get-tuple-element.8), kind=kLoop, calls=%fused_computation | loop fusion | flops 1572864 | bytes 2097152 | tf_op jit(solution)/shard_map/convert_element_type | solution.py:529
